TPU v7x, 128 devices: a whole 4x4x4 slice. The times are simulated.
128 devices in a mesh: ctx: 16 (over x, z_lo, core), tp: 8 (over z_hi, y).
Axes of the slice: x: 4, y: 4, z: 4 (z_hi: 2, z_lo: 2; z = z_hi * 2 + z_lo), core: 2. Of those that a mesh axis runs over, the one named last changes fastest.
Arguments:
- query_proj: bfloat16 [4096, 4096], P('ctx', 'tp'), may hold values from -220 to 220
- key_proj: bfloat16 [4096, 4096], P('ctx', 'tp'), may hold values from -6 to 6
- value_proj: bfloat16 [4096, 4096], P('ctx', 'tp'), may hold values from -6 to 6
- out_grad: bfloat16 [4096, 4096], P('ctx', 'tp'), may hold values from -6 to 6
- out_weight: bfloat16 [4096, 4096], P(None, 'tp'), may hold values from -0.125 to 0.125
- block_mask: int32 [32, 32], replicated, may hold values from 0 to 1, as said below
Outputs:
- query_grad: bfloat16 [4096, 4096], P('ctx', 'tp')
- key_grad: bfloat16 [4096, 4096], P('ctx', 'tp')
- value_grad: bfloat16 [4096, 4096], P('ctx', 'tp')
Inputs may be any that keep to these rules, and one draw needn't show every extreme that they name: block_mask[i, j] = 1 where blocks i and j belong to the same document or either of them is a global block, else 0; it is symmetric with ones on its diagonal.
All inputs are finite; a program needn't handle non-finite values.
Results may differ from a plain program's by a relative error of at most 0.02.
Values may be sent and summed in bfloat16 or wider, within the bound.
A program may use at most 192 MiB of HBM per device.

v0:
```python
import jax
import jax.numpy as jnp
from jax import lax
from jax.sharding import PartitionSpec as P

HEAD_DIM = 128
BLOCK = 128


NEG_FILL = -1e30


def by_heads(matrix):
    return matrix.reshape(matrix.shape[0], matrix.shape[1] // HEAD_DIM, HEAD_DIM)


def head_scores(query_heads, key_heads):
    return jnp.einsum(
        "qhd,khd->hqk", query_heads, key_heads, preferred_element_type=jnp.float32
    ) * HEAD_DIM ** (-0.5)


def pair_mask(block_mask, query_first, query_count, key_count):
    query_blocks = (query_first + jnp.arange(query_count, dtype=jnp.int32)) // BLOCK
    key_blocks = jnp.arange(key_count, dtype=jnp.int32) // BLOCK
    mask_rows = jnp.take(block_mask, query_blocks, axis=0)
    return jnp.take(mask_rows, key_blocks, axis=1) == 1


def tile_grads(query_heads, grad_heads, log_total, row_delta, key_heads, value_heads, allowed):
    scores = head_scores(query_heads, key_heads)
    probs = jnp.where(allowed[None], jnp.exp(scores - log_total[:, :, None]), 0.0)
    prob_grad = jnp.einsum(
        "qhd,khd->hqk", grad_heads, value_heads, preferred_element_type=jnp.float32
    )
    score_grad = (probs * (prob_grad - row_delta[:, :, None]) * HEAD_DIM ** (-0.5)).astype(
        jnp.bfloat16
    )
    return (probs.astype(jnp.bfloat16), score_grad)


def per_device(query_proj, key_proj, value_proj, out_grad, out_weight, block_mask):
    tok_rows, feat_width = query_proj.shape
    head_count = feat_width // HEAD_DIM
    grad_columns = lax.psum_scatter(
        lax.dot_general(
            out_weight, out_grad, (((1,), (1,)), ((), ())), preferred_element_type=jnp.float32
        ),
        "tp",
        scatter_dimension=0,
        tiled=True,
    )
    attn_grad = grad_columns.T.astype(jnp.bfloat16)
    first_row = lax.axis_index("ctx") * tok_rows
    query_heads = by_heads(query_proj)
    grad_heads = by_heads(attn_grad)
    key_piece = lax.all_gather(key_proj, "ctx", axis=0, tiled=True)
    value_piece = lax.all_gather(value_proj, "ctx", axis=0, tiled=True)
    piece_rows = key_piece.shape[0]
    allowed = pair_mask(block_mask, first_row, tok_rows, piece_rows)[None]
    scores = jnp.where(allowed, head_scores(query_heads, by_heads(key_piece)), NEG_FILL)
    prob_grad = jnp.einsum(
        "qhd,khd->hqk", grad_heads, by_heads(value_piece), preferred_element_type=jnp.float32
    )
    running_max = jnp.full((head_count, tok_rows), NEG_FILL, jnp.float32)
    new_max = jnp.maximum(running_max, jnp.max(scores, axis=2))
    weights = jnp.where(allowed, jnp.exp(scores - new_max[:, :, None]), 0.0)
    norm_total = jnp.sum(weights, axis=2)
    grad_total = jnp.sum(weights * prob_grad, axis=2)
    log_total = new_max + jnp.log(norm_total)
    row_delta = grad_total / norm_total
    key_piece = lax.all_gather(key_proj, "ctx", axis=0, tiled=True)
    value_piece = lax.all_gather(value_proj, "ctx", axis=0, tiled=True)
    piece_rows = key_piece.shape[0]
    key_heads = by_heads(key_piece)
    allowed = pair_mask(block_mask, first_row, tok_rows, piece_rows)
    prob_weights, score_grad = tile_grads(
        query_heads, grad_heads, log_total, row_delta, key_heads, by_heads(value_piece), allowed
    )
    query_acc = jnp.einsum(
        "hqk,khd->qhd", score_grad, key_heads, preferred_element_type=jnp.float32
    ).reshape(tok_rows, feat_width)
    key_part = jnp.einsum(
        "hqk,qhd->khd", score_grad, query_heads, preferred_element_type=jnp.float32
    ).reshape(piece_rows, feat_width)
    value_part = jnp.einsum(
        "hqk,qhd->khd", prob_weights, grad_heads, preferred_element_type=jnp.float32
    ).reshape(piece_rows, feat_width)
    updated = jnp.concatenate([key_part, value_part], axis=1)
    key_value_acc = updated
    query_acc, key_value_acc = (query_acc, key_value_acc)
    summed = lax.psum_scatter(
        key_value_acc.astype(jnp.bfloat16), "ctx", scatter_dimension=0, tiled=True
    ).astype(jnp.float32)
    key_acc = summed[:, :feat_width]
    value_acc = summed[:, feat_width:]
    return (
        query_acc.astype(jnp.bfloat16),
        key_acc.astype(jnp.bfloat16),
        value_acc.astype(jnp.bfloat16),
    )


def solution(mesh):
    placed = (P("ctx", "tp"), P("ctx", "tp"), P("ctx", "tp"), P("ctx", "tp"), P(None, "tp"), P())
    return jax.shard_map(
        per_device,
        mesh=mesh,
        in_specs=placed,
        out_specs=(P("ctx", "tp"), P("ctx", "tp"), P("ctx", "tp")),
        check_vma=False,
    )
```

profile of v0, /device:TPU:1, one launch (start us, length us, event | category | flops | bytes accessed | tf_op | source)
XLA Modules:
  0.0 292.0 jit_solution(18396936174778075570)
XLA Ops:
  8.1 1.8 copy.20
  10.0 5.4 %fusion.21 = f32[4096,256]{1,0:T(8,128)} fusion(bf16[4096,512]{1,0:T(8,128)(2,1)} %param.14, bf16[256,512]{1,0:T(8,128)(2,1)S(1)} %copy-done), kind=kOutput, calls=%fused_computation.44 | convolution fusion | flops 1073741824 | bytes 8650752 | tf_op jit(solution)/shard_map/dot_general | solution.py:46
  15.5 0.8 copy.23
  16.5 0.7 gather_fusion
  17.6 16.1 %gather_fusion.1 = s32[4096,256]{1,0:T(8,128)} fusion(s32[256,32]{0,1:T(8,128)S(1)} %copy.18, s32[4096]{0:T(1024)S(1)} %fusion.13), kind=kCustom, calls=%fused_computation.1.clone | custom fusion | bytes 8404992 | tf_op jit(solution)/shard_map/jit(_take)/gather | solution.py:27
  33.7 2.7 bitcast_compare_fusion
  36.4 2.4 copy.19
  38.9 25.7 %all-gather.3.cloned.1.call-done = bf16[4096,512]{0,1:T(8,128)(2,1)} async-done(((bf16[256,512]{0,1:T(8,128)(2,1)}), bf16[4096,512]{0,1:T(8,128)(2,1)}) %all-gather.3.cloned.1.call-update) | async-done | bytes 4194320 | tf_op jit(solution)/shard_map/all_gather | solution.py:72
  64.5 10.1 %select_reduce_fusion = (f32[4,256]{1,0:T(4,128)S(1)}, f32[4,256,4096]{2,1,0:T(8,128)}) fusion(pred[256,4096]{1,0:T(8,128)(4,1)S(1)} %copy.19, bf16[256,4,128]{0,2,1:T(8,128)(2,1)S(1)} %bitcast.32, bf16[4096,4,128]{0,2,1:T(8,128)(2,1)} %bitcast.29), kind=kOutput, calls=%fused_computation.6 | convolution fusion | flops 1086323712 | bytes 22286336 | tf_op jit(solution)/shard_map/qhd,khd->hqk/dot_general | solution.py:18
  74.6 33.0 %reduce-scatter.3.cloned.1.call-done = f32[512,256]{1,0:T(8,128)} async-done(((f32[4096,256]{1,0:T(8,128)}), f32[512,256]{1,0:T(8,128)}) %reduce-scatter.3.cloned.1.call-update) | async-done | bytes 524304 | tf_op jit(solution)/shard_map/reduce_scatter | solution.py:45
  107.6 1.1 convert_element_type.25
  108.7 10.6 %all-gather.5.cloned.1.call-done = bf16[4096,512]{0,1:T(8,128)(2,1)} async-done(((bf16[256,512]{0,1:T(8,128)(2,1)}), bf16[4096,512]{0,1:T(8,128)(2,1)}) %all-gather.5.cloned.1.call-update) | async-done | bytes 4194320 | tf_op jit(solution)/shard_map/all_gather | solution.py:73
  119.3 15.6 %fusion.1 = (f32[4,256]{1,0:T(4,128)S(1)}, f32[4,256]{1,0:T(4,128)S(1)}, f32[4,256,4096]{2,1,0:T(8,128)}) fusion(f32[4,256,4096]{2,1,0:T(8,128)} %get-tuple-element.18, f32[4,256]{1,0:T(4,128)S(1)} %broadcast_maximum_fusion, pred[256,4096]{1,0:T(8,128)(4,1)S(1)} %copy.19, bf16[256,4,128]{0,2,1:T(8,128)(2,1)S(1)} %bitcast.34, bf16[4096,4,128]{0,2,1:T(8,128)(2,1)} %bitcast.37), kind=kOutput, calls=%fused_computation.8 | convolution fusion | flops 1103099904 | bytes 39071744 | tf_op jit(solution)/shard_map/qhd,khd->hqk/dot_general | solution.py:33
  134.9 11.8 %fusion.8 = bf16[4,128,4096]{2,1,0:T(8,128)(2,1)} fusion(bf16[256,4,128]{0,2,1:T(8,128)(2,1)S(1)} %bitcast.35, f32[4,256,4096]{2,1,0:T(8,128)} %get-tuple-element.18, f32[4,256]{1,0:T(4,128)S(1)} %get-tuple-element.15, pred[256,4096]{1,0:T(8,128)(4,1)S(1)} %copy.19), kind=kOutput, calls=%fused_computation.16 | convolution fusion | flops 1092616192 | bytes 22286336 | tf_op jit(solution)/shard_map/hqk,qhd->khd/dot_general | solution.py:86
  146.7 12.4 %multiply_convert_fusion = bf16[4,256,4096]{2,1,0:T(8,128)(2,1)S(1)} fusion(f32[4,256,4096]{2,1,0:T(8,128)} %get-tuple-element.19, f32[4,256,4096]{2,1,0:T(8,128)} %get-tuple-element.18, f32[4,256]{1,0:T(4,128)S(1)} %get-tuple-element.16, f32[4,256]{1,0:T(4,128)S(1)} %get-tuple-element.15, pred[256,4096]{1,0:T(8,128)(4,1)S(1)} %copy.19), kind=kLoop, calls=%fused_computation.2 | loop fusion | flops 29360128 | bytes 42999808 | tf_op jit(solution)/shard_map/convert_element_type | solution.py:36
  159.1 3.2 %copy-done.3 = bf16[4,256,4096]{2,1,0:T(8,128)(2,1)} copy-done((bf16[4,256,4096]{2,1,0:T(8,128)(2,1)}, bf16[4,256,4096]{2,1,0:T(8,128)(2,1)S(1)}, u32[]{:S(2)}) %copy-start.3) | copy-done | bytes 8388632
  162.3 3.2 %convolution_convert_fusion = bf16[4,4096,128]{1,2,0:T(8,128)(2,1)} fusion(bf16[256,4,128]{0,2,1:T(8,128)(2,1)S(1)} %bitcast.33, bf16[4,256,4096]{2,1,0:T(8,128)(2,1)S(1)} %multiply_convert_fusion), kind=kOutput, calls=%fused_computation.15 | convolution fusion | flops 1075838976 | bytes 12845056 | tf_op jit(solution)/shard_map/hqk,qhd->khd/dot_general | solution.py:83
  165.6 6.5 %copy.27 = bf16[4096,512]{1,0:T(8,128)(2,1)} copy(bf16[4096,512]{0,1:T(8,128)(2,1)} %bitcast.28) | data formatting | bytes 8388608 | tf_op jit(solution)/shard_map/reshape | solution.py:85
  172.1 6.5 %copy.28 = bf16[4096,512]{1,0:T(8,128)(2,1)} copy(bf16[4096,512]{0,1:T(8,128)(2,1)} %bitcast.31) | data formatting | bytes 8388608 | tf_op jit(solution)/shard_map/reshape | solution.py:88
  178.6 7.9 %pad_maximum_fusion = bf16[4096,1024]{1,0:T(8,128)(2,1)} fusion(bf16[4096,512]{1,0:T(8,128)(2,1)} %copy.28, bf16[4096,512]{1,0:T(8,128)(2,1)} %copy.27), kind=kLoop, calls=%fused_computation.10 | loop fusion | flops 16777216 | bytes 16777216 | tf_op jit(solution)/shard_map/concatenate | solution.py:89
  186.5 7.5 %convolution_convert_fusion.1 = bf16[4,256,128]{1,2,0:T(8,128)(2,1)S(1)} fusion(bf16[4,256,4096]{2,1,0:T(8,128)(2,1)} %copy-done.3, bf16[4096,4,128]{0,2,1:T(8,128)(2,1)} %bitcast.30), kind=kOutput, calls=%fused_computation.18 | convolution fusion | flops 1073872896 | bytes 12845056 | tf_op jit(solution)/shard_map/hqk,khd->qhd/dot_general | solution.py:80
  194.0 0.8 copy.29
  194.9 88.2 %reduce-scatter.5.cloned.1.call-done = bf16[256,1024]{1,0:T(8,128)(2,1)} async-done(((bf16[4096,1024]{1,0:T(8,128)(2,1)}), bf16[256,1024]{1,0:T(8,128)(2,1)}) %reduce-scatter.5.cloned.1.call-update) | async-done | bytes 524304 | tf_op jit(solution)/shard_map/reduce_scatter | solution.py:92
  283.0 1.9 fusion.20
  (29 shorter events, 0.6 us)
Async XLA Ops:
  8.0 2.0 copy-start
  8.0 7.5 %copy-start.4 = (bf16[256,512]{1,0:T(8,128)(2,1)S(1)}, bf16[256,512]{1,0:T(8,128)(2,1)}, u32[]{:S(2)}) copy-start(bf16[256,512]{1,0:T(8,128)(2,1)} %param.12) | copy-start | bytes 786436
  8.0 8.5 %copy-start.2 = (s32[32,32]{1,0:T(8,128)S(1)}, s32[32,32]{1,0:T(8,128)}, u32[]{:S(2)}) copy-start(s32[32,32]{1,0:T(8,128)} %param.15) | copy-start | bytes 12292
  8.0 56.5 %all-gather.3.cloned.1.call-start = ((), (), s32[]{:S(2)}) async-start(), calls=%async_computation.2 | async-start | bytes 4456448 | tf_op jit(solution)/shard_map/all_gather | solution.py:72
  9.9 7.5 %copy-start.5 = (bf16[256,512]{1,0:T(8,128)(2,1)S(1)}, bf16[256,512]{1,0:T(8,128)(2,1)}, u32[]{:S(2)}) copy-start(bf16[256,512]{1,0:T(8,128)(2,1)} %param.10) | copy-start | bytes 786436
  10.0 97.7 %reduce-scatter.3.cloned.1.call-start = ((), (), s32[]{:S(2)}) async-start(), calls=%async_computation.3 | async-start | bytes 4718592 | tf_op jit(solution)/shard_map/reduce_scatter | solution.py:45
  15.5 103.8 %all-gather.5.cloned.1.call-start = ((), (), s32[]{:S(2)}) async-start(), calls=%async_computation.4 | async-start | bytes 4456448 | tf_op jit(solution)/shard_map/all_gather | solution.py:73
  16.4 266.6 %reduce-scatter.5.cloned.1.call-start = ((), (), s32[]{:S(2)}) async-start(), calls=%async_computation.5 | async-start | bytes 8912896 | tf_op jit(solution)/shard_map/reduce_scatter | solution.py:92
  159.1 3.2 %copy-start.3 = (bf16[4,256,4096]{2,1,0:T(8,128)(2,1)}, bf16[4,256,4096]{2,1,0:T(8,128)(2,1)S(1)}, u32[]{:S(2)}) copy-start(bf16[4,256,4096]{2,1,0:T(8,128)(2,1)S(1)} %multiply_convert_fusion) | copy-start | bytes 25165828
  186.5 98.4 %copy-start.1 = (bf16[256,512]{1,0:T(8,128)(2,1)S(1)}, bf16[256,512]{1,0:T(8,128)(2,1)}, u32[]{:S(2)}) copy-start(bf16[256,512]{1,0:T(8,128)(2,1)} %param.13) | copy-start | bytes 786436
Sparse Core Ops, SparseCore 0:
  11.1 53.4 all-gather.2
  66.7 52.4 all-gather.4
  186.6 96.3 reduce-scatter.4
Sparse Core Ops, SparseCore 1:
  15.6 92.0 reduce-scatter.2
where the time goes:
time: 293 us; the launch traced here: 292 us
  waiting for transfers between devices  157 us (54%)
  matrix products  53.7 us (18%)
  local copies, waits for them, and re-layouts  41.1 us (14%)
  other arithmetic  24.2 us (8%)
  between operations  15.3 us (5%)
    reduce_scatter x1, waiting for transfers between devices, per_device(): lax.psum_scatter(key_value_acc.astype(jnp.bfloat16), 'ctx', scatter_dimen...  88.2 us
    reduce_scatter x1, waiting for transfers between devices, per_device(): lax.psum_scatter(lax.dot_general(out_weight, out_grad, (((1,), (1,)), (()...  33 us
    all_gather x1, waiting for transfers between devices, per_device(): key_piece = lax.all_gather(key_proj, 'ctx', axis=0, tiled=True)  25.7 us
    gather x1, local copies, waits for them, and re-layouts, pair_mask(): return jnp.take(mask_rows, key_blocks, axis=1) == 1  16.1 us
    dot_general x1, matrix products, tile_grads(): jnp.einsum('qhd,khd->hqk', grad_heads, value_heads, preferred_element_typ...  15.6 us
    convert_element_type x1, other arithmetic, tile_grads(): (probs * (prob_grad - row_delta[:, :, None]) * HEAD_DIM ** (-0.5)).astype...  12.4 us
    dot_general x1, matrix products, per_device(): jnp.einsum('hqk,qhd->khd', prob_weights, grad_heads, preferred_element_ty...  11.8 us
    all_gather x1, waiting for transfers between devices, per_device(): value_piece = lax.all_gather(value_proj, 'ctx', axis=0, tiled=True)  10.6 us
  transfers between devices with their start and end apart: 4, of which 4 were waited for; matrix products, arithmetic and copies ran while one was open for 16% of the time, Pallas kernels for 0%

commit v1 on v0

v1 whole, which is shorter than its diff:
```python
import functools

import jax
import jax.numpy as jnp
from jax import lax
from jax.experimental import pallas as pl
from jax.experimental.pallas import tpu as pltpu
from jax.sharding import PartitionSpec as P

MESH = pl.DeviceIdType.MESH
HEAD_DIM = 128
BLOCK = 128
ROWS = 256
NX = 4
NEG_FILL = -1e30
SCALE = HEAD_DIM ** (-0.5)
LOG2E = 1.4426950408889634
BF16 = jnp.bfloat16
F32 = jnp.float32
NT = (((1,), (1,)), ((), ()))


def place():
    ctx, tp = lax.axis_index("ctx"), lax.axis_index("tp")
    return (
        lax.div(ctx, 4),
        lax.rem(lax.div(ctx, 2), 2),
        lax.rem(ctx, 2),
        lax.div(tp, 4),
        lax.rem(tp, 4),
    )


def device(x, z, c, zh, y):
    return {"ctx": x * 4 + z * 2 + c, "tp": zh * 4 + y}


def block_rows(x, z, c):
    return pl.ds(pl.multiple_of((x * 4 + z * 2 + c) * ROWS, ROWS), ROWS)


def head_lanes(h):
    return pl.ds(pl.multiple_of(h * HEAD_DIM, HEAD_DIM), HEAD_DIM)


def remote(src, dst, send, recv, to):
    return pltpu.make_async_remote_copy(
        src_ref=src, dst_ref=dst, send_sem=send, recv_sem=recv, device_id=to, device_id_type=MESH
    )


def spread_kernel(
    q_in, k_in, v_in, og_in, w_in,
    q_out, k_out, v_out, g_out,
    og, w, own, relay, relay_got, comb, comb_got, direct, direct_got, z_part, z_got, g_part,
    load_sem, local_sem, y_send, y_recv, z_send, z_recv, g_send, g_recv,
    q_send, q_recv, kv_xsend, kv_xrecv, kv_fsend, kv_frecv,
):
    x, z, c, zh, y = place()
    yp, ym, yo = lax.rem(y + 1, 4), lax.rem(y + 3, 4), lax.rem(y + 2, 4)

    def at_x(d):
        return device(lax.rem(x + d, 4), z, c, zh, y)

    core, zpeer = device(x, z, 1 - c, zh, y), device(x, 1 - z, c, zh, y)
    up, down = device(x, z, c, zh, yp), device(x, z, c, zh, ym)
    zfar = device(x, z, c, 1 - zh, y)

    order = [(yo, 0), (yo, 1), (yp, 0), (ym, 1), (yp, 1), (ym, 0), (y, 0), (y, 1)]
    loads = [pltpu.make_async_copy(og_in, og, load_sem.at[8])]
    for i, (yy, zz) in enumerate(order):
        rows = pl.ds(pl.multiple_of((zz * 4 + yy) * 512, 512), 512)
        loads.append(pltpu.make_async_copy(w_in.at[rows], w.at[i], load_sem.at[i]))
    for load in loads:
        load.start()

    barrier = pltpu.get_barrier_semaphore()
    for peer in (at_x(1), at_x(2), at_x(3), core, zpeer, up, down, zfar):
        pl.semaphore_signal(barrier, inc=1, device_id=peer, device_id_type=MESH)
    pl.semaphore_wait(barrier, 8)

    sent = []

    def go(copy):
        copy.start()
        sent.append(copy)

    def project(i):
        loads[1 + i].wait()
        return lax.dot_general(og[...], w[i], NT, preferred_element_type=F32)

    heads = [lax.rem(x + 1 + i, 4) for i in range(4)]

    def y_copy(kind, zz, i, src, dst, to):
        return remote(
            src.at[zz, heads[i]], dst.at[zz, heads[i]],
            y_send.at[kind, zz, i], y_recv.at[kind, zz, i], to,
        )

    loads[0].wait()
    for zz in range(2):
        part = project(zz)
        for h in range(4):
            relay[zz, h] = part[:, h * 128:(h + 1) * 128].astype(BF16)
    relays = [[y_copy(0, zz, i, relay, relay_got, (up, down)[zz]) for i in range(4)] for zz in range(2)]
    for i in range(4):
        for zz in range(2):
            go(relays[zz][i])

    tensors = [(k_in, k_out), (v_in, v_out)]

    def kv_from_x(t, d):
        src, dst = tensors[t]
        return remote(
            src.at[:, head_lanes(lax.rem(x + d, 4))], dst.at[block_rows(x, z, c)],
            kv_xsend.at[t, d], kv_xrecv.at[t, d], at_x(d),
        )

    def kv_wait_x(t, d):
        dst = tensors[t][1].at[block_rows(lax.rem(x + 4 - d, 4), z, c)]
        remote(dst, dst, kv_xsend.at[t, d], kv_xrecv.at[t, d], core).wait_recv()

    def kv_forward(t, d, route):
        xs = lax.rem(x + 4 - d, 4)
        rows = block_rows(xs, z if route < 2 else 1 - z, c)
        dst = tensors[t][1].at[rows]
        src = tensors[t][0].at[:, head_lanes(x)] if (d == 0 and route < 2) else dst
        return remote(
            src, dst, kv_fsend.at[t, d, route], kv_frecv.at[t, d, route], zpeer if route == 1 else core
        )

    def kv_wait(t, d, route):
        xs = lax.rem(x + 4 - d, 4)
        rows = block_rows(xs, z if route == 0 else 1 - z, c if route == 1 else 1 - c)
        dst = tensors[t][1].at[rows]
        remote(dst, dst, kv_fsend.at[t, d, route], kv_frecv.at[t, d, route], core).wait_recv()

    for t in range(2):
        go(kv_forward(t, 0, 1))
    for d in (1, 3, 2):
        for t in range(2):
            go(kv_from_x(t, d))
    for t in range(2):
        go(kv_forward(t, 0, 0))
    local = []
    for t in range(2):
        local.append(pltpu.make_async_copy(
            tensors[t][0].at[:, head_lanes(x)], tensors[t][1].at[block_rows(x, z, c)], local_sem.at[t]))
    q_rows = pl.ds(pl.multiple_of(x * ROWS, ROWS), ROWS)
    local.append(pltpu.make_async_copy(q_in.at[:, head_lanes(x)], q_out.at[q_rows], local_sem.at[2]))
    for copy in local:
        copy.start()
    q_copies = [
        remote(q_in.at[:, head_lanes(lax.rem(x + d, 4))], q_out.at[q_rows], q_send.at[d], q_recv.at[d], at_x(d))
        for d in (1, 2, 3)
    ]

    for i in range(2, 8):
        zz = order[i][1]
        part = project(i)
        for h in range(4):
            piece = part[:, h * 128:(h + 1) * 128]
            if i in (4, 5):
                direct[zz, h] = piece.astype(BF16)
            else:
                own[0 if i < 4 else 1, zz, h] = piece

    def combine(i):
        h = heads[i]
        for zz in range(2):
            relays[zz][i].wait_recv()
            comb[zz, h] = (relay_got[zz, h].astype(F32) + own[0, zz, h]).astype(BF16)
            go(y_copy(1, zz, i, comb, comb_got, (up, down)[zz]))
        for zz in range(2):
            go(y_copy(2, zz, i, direct, direct_got, (down, up)[zz]))

    z_copies = [
        remote(z_part.at[heads[i]], z_got.at[heads[i]], z_send.at[i], z_recv.at[i], zfar) for i in range(4)
    ]

    def finish_y(i):
        h = heads[i]
        for zz in range(2):
            y_copy(1, zz, i, comb, comb_got, up).wait_recv()
            y_copy(2, zz, i, direct, direct_got, up).wait_recv()
        far = own[1, 1 - zh, h] + comb_got[1 - zh, h].astype(F32) + direct_got[1 - zh, h].astype(F32)
        z_part[h] = far.astype(BF16)
        go(z_copies[i])
        own[1, zh, h] = own[1, zh, h] + comb_got[zh, h].astype(F32) + direct_got[zh, h].astype(F32)

    def finish_z(i):
        h = heads[i]
        z_copies[i].wait_recv()
        g_part[h] = (own[1, zh, h] + z_got[h].astype(F32)).astype(BF16)
        if i < 3:
            go(remote(g_part.at[h], g_out.at[q_rows], g_send.at[i], g_recv.at[i], at_x(i + 1)))
        else:
            copy = pltpu.make_async_copy(g_part.at[h], g_out.at[q_rows], local_sem.at[3])
            copy.start()
            local.append(copy)

    def pass_on(d):
        for t in range(2):
            kv_wait_x(t, d)
            go(kv_forward(t, d, 1))
            go(kv_forward(t, d, 0))

    def pass_z(d):
        for t in range(2):
            kv_wait(t, d, 1)
            go(kv_forward(t, d, 2))

    combine(0)
    pass_on(1)
    combine(1)
    pass_on(3)
    for copy in q_copies:
        go(copy)
    combine(2)
    pass_z(0)
    combine(3)
    pass_on(2)
    pass_z(1)
    finish_y(0)
    pass_z(3)
    finish_y(1)
    finish_z(0)
    finish_y(2)
    finish_z(1)
    pass_z(2)
    finish_y(3)
    finish_z(2)
    finish_z(3)

    for d in range(4):
        for t in range(2):
            kv_wait(t, d, 0)
            kv_wait(t, d, 2)
    for copy in q_copies:
        copy.wait_recv()
    for i in range(3):
        rows = pl.ds(pl.multiple_of(lax.rem(x + 3 - i, 4) * ROWS, ROWS), ROWS)
        dst = g_out.at[rows]
        remote(dst, dst, g_send.at[i], g_recv.at[i], core).wait_recv()
    for copy in local:
        copy.wait()
    for copy in sent:
        copy.wait_send()


def spread(q, k, v, og, w):
    dma = pltpu.SemaphoreType.DMA
    hbm = pl.BlockSpec(memory_space=pltpu.HBM)
    return pl.pallas_call(
        spread_kernel,
        out_shape=(
            jax.ShapeDtypeStruct((NX * ROWS, 128), BF16),
            jax.ShapeDtypeStruct((16 * ROWS, 128), BF16),
            jax.ShapeDtypeStruct((16 * ROWS, 128), BF16),
            jax.ShapeDtypeStruct((NX * ROWS, 128), BF16),
        ),
        in_specs=[hbm] * 5,
        out_specs=(hbm,) * 4,
        scratch_shapes=[
            pltpu.VMEM((ROWS, 512), BF16),
            pltpu.VMEM((8, 512, 512), BF16),
            pltpu.VMEM((2, 2, 4, ROWS, 128), F32),
            *[pltpu.VMEM((2, 4, ROWS, 128), BF16)] * 6,
            *[pltpu.VMEM((4, ROWS, 128), BF16)] * 3,
            dma((9,)), dma((4,)),
            dma((3, 2, 4)), dma((3, 2, 4)),
            dma((4,)), dma((4,)), dma((3,)), dma((3,)),
            dma((4,)), dma((4,)),
            dma((2, 4)), dma((2, 4)), dma((2, 4, 3)), dma((2, 4, 3)),
        ],
        compiler_params=pltpu.CompilerParams(
            collective_id=0, has_side_effects=True, vmem_limit_bytes=48 << 20
        ),
        name="spread",
    )(q, k, v, og, w)


GROUP = 4


def attention_kernel(mask, q, g, k, v, dq, dk, dv, s_scr, p_scr, dk_acc, dv_acc, picks, bias):
    ctx = lax.axis_index("ctx")
    zc = lax.rem(ctx, 4)
    dk_acc[...] = jnp.zeros_like(dk_acc)
    dv_acc[...] = jnp.zeros_like(dv_acc)

    def tile(i, carry):
        first = (i * 4 + zc) * 2
        def pick(b, count):
            m0, m1 = mask[first, b] == 1, mask[first + 1, b] == 1
            picks[count] = b
            bias[0, count] = jnp.where(m0, 0.0, NEG_FILL)
            bias[1, count] = jnp.where(m1, 0.0, NEG_FILL)
            return count + jnp.where(m0 | m1, 1, 0)

        count = lax.fori_loop(0, 32, pick, 0)
        steps = lax.div(count + GROUP - 1, GROUP)

        def pad(b, carry):
            picks[b] = 0
            bias[0, b] = NEG_FILL
            bias[1, b] = NEG_FILL
            return carry

        lax.fori_loop(count, steps * GROUP, pad, 0)

        q_rows = pl.ds(pl.multiple_of(i * ROWS, ROWS), ROWS)
        q_tile, g_tile = q[q_rows, :], g[q_rows, :]

        def rows_of(j, n):
            return pl.ds(pl.multiple_of(picks[j * GROUP + n] * BLOCK, BLOCK), BLOCK)

        def scores(j, top):
            k_cat = jnp.concatenate([k[rows_of(j, n), :] for n in range(GROUP)], axis=0)
            v_cat = jnp.concatenate([v[rows_of(j, n), :] for n in range(GROUP)], axis=0)
            s = lax.dot_general(k_cat, q_tile, NT, preferred_element_type=F32)
            p_scr[j] = lax.dot_general(v_cat, g_tile, NT, preferred_element_type=F32)
            for n in range(GROUP):
                fill = jnp.concatenate(
                    [jnp.full((1, 128), bias[a, j * GROUP + n], F32) for a in range(2)], axis=1
                )
                part = s[n * BLOCK:(n + 1) * BLOCK] * (SCALE * LOG2E) + fill
                s_scr[j, n * BLOCK:(n + 1) * BLOCK, :] = part
                top = jnp.maximum(top, jnp.max(part.reshape(BLOCK // 8, 8, ROWS), axis=0))
            return top

        top = lax.fori_loop(0, steps, scores, jnp.full((8, ROWS), NEG_FILL, F32))
        top = jnp.max(top, axis=0, keepdims=True)

        def sums(j, carry):
            total, weighted = carry
            e = jnp.exp2(s_scr[j] - top)
            s_scr[j] = e
            total = total + jnp.sum(e.reshape(GROUP * BLOCK // 8, 8, ROWS), axis=0)
            weighted = weighted + jnp.sum((e * p_scr[j]).reshape(GROUP * BLOCK // 8, 8, ROWS), axis=0)
            return total, weighted

        zero = jnp.zeros((8, ROWS), F32)
        total, weighted = lax.fori_loop(0, steps, sums, (zero, zero))
        inverse = 1.0 / jnp.sum(total, axis=0, keepdims=True)
        delta = jnp.sum(weighted, axis=0, keepdims=True) * inverse

        def grads(j, dq_acc):
            p = s_scr[j] * inverse
            ds = (p * (p_scr[j] - delta)).astype(BF16)
            p = p.astype(BF16)
            k_cat = jnp.concatenate([k[rows_of(j, n), :] for n in range(GROUP)], axis=0)
            dv_part = jnp.dot(p, g_tile, preferred_element_type=F32)
            dk_part = jnp.dot(ds, q_tile, preferred_element_type=F32)
            dq_acc = dq_acc + lax.dot_general(
                ds, k_cat, (((0,), (0,)), ((), ())), preferred_element_type=F32
            )
            for n in range(GROUP):
                rows = rows_of(j, n)
                dk_acc[rows, :] += dk_part[n * BLOCK:(n + 1) * BLOCK]
                dv_acc[rows, :] += dv_part[n * BLOCK:(n + 1) * BLOCK]
            return dq_acc

        dq_acc = lax.fori_loop(0, steps, grads, jnp.zeros((ROWS, 128), F32))
        dq[q_rows, :] = (dq_acc * SCALE).astype(BF16)
        return carry

    lax.fori_loop(0, NX, tile, 0)
    dk[...] = (dk_acc[...] * SCALE).astype(BF16)
    dv[...] = dv_acc[...].astype(BF16)


def attention(mask, q, g, k, v):
    vmem = pl.BlockSpec(memory_space=pltpu.VMEM)
    return pl.pallas_call(
        attention_kernel,
        out_shape=(
            jax.ShapeDtypeStruct((NX * ROWS, 128), BF16),
            jax.ShapeDtypeStruct((16 * ROWS, 128), BF16),
            jax.ShapeDtypeStruct((16 * ROWS, 128), BF16),
        ),
        in_specs=[pl.BlockSpec(memory_space=pltpu.SMEM)] + [vmem] * 4,
        out_specs=(vmem,) * 3,
        scratch_shapes=[
            pltpu.VMEM((32 // GROUP, GROUP * BLOCK, ROWS), F32),
            pltpu.VMEM((32 // GROUP, GROUP * BLOCK, ROWS), F32),
            pltpu.VMEM((16 * ROWS, 128), F32),
            pltpu.VMEM((16 * ROWS, 128), F32),
            pltpu.SMEM((64,), jnp.int32),
            pltpu.SMEM((2, 64), F32),
        ],
        compiler_params=pltpu.CompilerParams(vmem_limit_bytes=48 << 20),
        name="attention",
    )(mask, q, g, k, v)


def collect_kernel(
    dq_in, dk_in, dv_in,
    dq_out, dk_out, dv_out,
    own, core_got, z_part, z_got, part,
    load_sem, local_sem, core_send, core_recv, z_send, z_recv, x_send, x_recv, q_send, q_recv,
):
    x, z, c, zh, y = place()

    def at_x(d):
        return device(lax.rem(x + d, 4), z, c, zh, y)

    core, zpeer = device(x, z, 1 - c, zh, y), device(x, 1 - z, c, zh, y)
    tensors = [(dk_in, dk_out), (dv_in, dv_out)]
    order = (1, 3, 2, 0)

    loads = {}
    for far in (1, 0):
        for d in order:
            for t in range(2):
                rows = block_rows(lax.rem(x + d, 4), 1 - z if far else z, c)
                loads[far, d, t] = pltpu.make_async_copy(
                    tensors[t][0].at[rows], own.at[far, d, t], load_sem.at[far, d, t])
                loads[far, d, t].start()

    barrier = pltpu.get_barrier_semaphore()
    for peer in (at_x(1), at_x(2), at_x(3), core, zpeer):
        pl.semaphore_signal(barrier, inc=1, device_id=peer, device_id_type=MESH)
    pl.semaphore_wait(barrier, 5)

    sent = []

    def go(copy):
        copy.start()
        sent.append(copy)

    to_core = {}
    for far in (1, 0):
        for d in order:
            for t in range(2):
                rows = block_rows(lax.rem(x + d, 4), 1 - z if far else z, 1 - c)
                to_core[far, d, t] = remote(
                    tensors[t][0].at[rows], core_got.at[far, d, t],
                    core_send.at[far, d, t], core_recv.at[far, d, t], core)
                go(to_core[far, d, t])

    q_copies = [
        remote(
            dq_in.at[pl.ds(pl.multiple_of(lax.rem(x + d, 4) * ROWS, ROWS), ROWS)],
            dq_out.at[:, head_lanes(x)], q_send.at[d], q_recv.at[d], at_x(d))
        for d in (1, 2, 3)
    ]
    for copy in q_copies:
        go(copy)
    local = [pltpu.make_async_copy(
        dq_in.at[pl.ds(pl.multiple_of(x * ROWS, ROWS), ROWS)], dq_out.at[:, head_lanes(x)], local_sem.at[2])]
    local[0].start()

    to_z = {}
    for d in order:
        for t in range(2):
            loads[1, d, t].wait()
            to_core[1, d, t].wait_recv()
            z_part[d, t] = (own[1, d, t].astype(F32) + core_got[1, d, t].astype(F32)).astype(BF16)
            to_z[d, t] = remote(z_part.at[d, t], z_got.at[d, t], z_send.at[d, t], z_recv.at[d, t], zpeer)
            go(to_z[d, t])
    for d in order:
        for t in range(2):
            loads[0, d, t].wait()
            to_core[0, d, t].wait_recv()
            to_z[d, t].wait_recv()
            part[d, t] = (
                own[0, d, t].astype(F32) + core_got[0, d, t].astype(F32) + z_got[d, t].astype(F32)
            ).astype(BF16)
            dst = tensors[t][1].at[:, head_lanes(x)]
            if d == 0:
                copy = pltpu.make_async_copy(part.at[d, t], dst, local_sem.at[t])
                copy.start()
                local.append(copy)
            else:
                go(remote(part.at[d, t], dst, x_send.at[d, t], x_recv.at[d, t], at_x(d)))

    for d in (1, 2, 3):
        lanes = head_lanes(lax.rem(x + 4 - d, 4))
        for t in range(2):
            dst = tensors[t][1].at[:, lanes]
            remote(dst, dst, x_send.at[d, t], x_recv.at[d, t], core).wait_recv()
        dst = dq_out.at[:, lanes]
        remote(dst, dst, q_send.at[d], q_recv.at[d], core).wait_recv()
    for copy in local:
        copy.wait()
    for copy in sent:
        copy.wait_send()


def collect(dq, dk, dv):
    dma = pltpu.SemaphoreType.DMA
    hbm = pl.BlockSpec(memory_space=pltpu.HBM)
    piece = (ROWS, 128)
    return pl.pallas_call(
        collect_kernel,
        out_shape=(jax.ShapeDtypeStruct((ROWS, 512), BF16),) * 3,
        in_specs=[hbm] * 3,
        out_specs=(hbm,) * 3,
        scratch_shapes=[
            pltpu.VMEM((2, 4, 2, *piece), BF16),
            pltpu.VMEM((2, 4, 2, *piece), BF16),
            pltpu.VMEM((4, 2, *piece), BF16),
            pltpu.VMEM((4, 2, *piece), BF16),
            pltpu.VMEM((4, 2, *piece), BF16),
            dma((2, 4, 2)), dma((3,)),
            dma((2, 4, 2)), dma((2, 4, 2)),
            dma((4, 2)), dma((4, 2)),
            dma((4, 2)), dma((4, 2)),
            dma((4,)), dma((4,)),
        ],
        compiler_params=pltpu.CompilerParams(
            collective_id=1, has_side_effects=True, vmem_limit_bytes=48 << 20
        ),
        name="collect",
    )(dq, dk, dv)


def per_device(query_proj, key_proj, value_proj, out_grad, out_weight, block_mask):
    q, k, v, g = spread(query_proj, key_proj, value_proj, out_grad, out_weight)
    dq, dk, dv = attention(block_mask, q, g, k, v)
    return collect(dq, dk, dv)


def solution(mesh):
    placed = (P("ctx", "tp"), P("ctx", "tp"), P("ctx", "tp"), P("ctx", "tp"), P(None, "tp"), P())
    return jax.shard_map(
        per_device,
        mesh=mesh,
        in_specs=placed,
        out_specs=(P("ctx", "tp"), P("ctx", "tp"), P("ctx", "tp")),
        check_vma=False,
    )
```

time: 293 us -> 79.6 us (0.27)
  waiting for transfers between devices: 157 us -> 0 us
  Pallas kernels: 0 us -> 72.8 us
  matrix products: 53.7 us -> 0 us
  local copies, waits for them, and re-layouts: 41.1 us -> 5.9 us
  other arithmetic: 24.2 us -> 0 us
  between operations: 15.3 us -> 0.68 us
    reduce_scatter x2 -> x0, waiting for transfers between devices: 121 us -> none  [the longest x1 88.2 us: per_device(): lax.psum_scatter(key_value_acc.astype(jnp.bfloat16), 'ctx', scatter_dimen...]
    pallas_call x0 -> x3, Pallas kernels: none -> 72.8 us  [the longest x1 31.7 us: spread(): pl.pallas_call(spread_kernel, out_shape=(jax.ShapeDtypeStruct((NX * ROWS,...]
    dot_general x6 -> x0, matrix products: 53.7 us -> none  [the longest x1 15.6 us: tile_grads(): jnp.einsum('qhd,khd->hqk', grad_heads, value_heads, preferred_element_typ...]
    all_gather x2 -> x0, waiting for transfers between devices: 36.2 us -> none  [the longest x1 25.7 us: per_device(): key_piece = lax.all_gather(key_proj, 'ctx', axis=0, tiled=True)]
    gather x2 -> x0, local copies, waits for them, and re-layouts: 16.8 us -> none  [the longest x1 16.1 us: pair_mask(): return jnp.take(mask_rows, key_blocks, axis=1) == 1]
    convert_element_type x2 -> x0, other arithmetic: 13.5 us -> none  [the longest x1 12.4 us: tile_grads(): (probs * (prob_grad - row_delta[:, :, None]) * HEAD_DIM ** (-0.5)).astype...]
    reshape x3 -> x0, local copies, waits for them, and re-layouts: 13.1 us -> none  [the longest x1 6.5 us: per_device(): value_part = jnp.einsum('hqk,qhd->khd', prob_weights, grad_heads, preferr...]
    concatenate x1 -> x0, other arithmetic: 7.86 us -> none  [per_device(): updated = jnp.concatenate([key_part, value_part], axis=1)]
  transfers between devices with their start and end apart: 4 -> 0, of which waited for: 4 -> 0; matrix products, arithmetic and copies ran while one was open for 16% -> 0% of each run, Pallas kernels for 0% -> 0%
where the time goes in v1:
time: 79.6 us; the launch traced here: 79.4 us
  Pallas kernels  72.8 us (91%)
  local copies, waits for them, and re-layouts  5.9 us (7%)
    pallas_call x1, Pallas kernels, spread(): pl.pallas_call(spread_kernel, out_shape=(jax.ShapeDtypeStruct((NX * ROWS,...  31.7 us
    pallas_call x1, Pallas kernels, collect(): pl.pallas_call(collect_kernel, out_shape=(jax.ShapeDtypeStruct((ROWS, 512...  29.4 us
    pallas_call x1, Pallas kernels, attention(): pl.pallas_call(attention_kernel, out_shape=(jax.ShapeDtypeStruct((NX * RO...  11.7 us
    unnamed x13, local copies, waits for them, and re-layouts  5.9 us

profile of v1, /device:TPU:1, one launch (start us, length us, event | category | flops | bytes accessed | tf_op | source)
XLA Modules:
  0.0 79.4 jit_solution(17424970369320275430)
XLA Ops:
  0.6 0.0 copy-start
  0.6 0.9 %copy-done = bf16[256,512]{1,0:T(8,128)(2,1)S(1)} copy-done((bf16[256,512]{1,0:T(8,128)(2,1)S(1)}, bf16[256,512]{1,0:T(8,128)(2,1)}, u32[]{:S(2)}) %copy-start) | copy-done | bytes 262168
  1.6 0.0 copy-start.1
  1.6 0.9 %copy-done.1 = bf16[256,512]{1,0:T(8,128)(2,1)S(1)} copy-done((bf16[256,512]{1,0:T(8,128)(2,1)S(1)}, bf16[256,512]{1,0:T(8,128)(2,1)}, u32[]{:S(2)}) %copy-start.1) | copy-done | bytes 262168
  2.5 0.0 copy-start.2
  2.5 0.9 %copy-done.2 = bf16[256,512]{1,0:T(8,128)(2,1)S(1)} copy-done((bf16[256,512]{1,0:T(8,128)(2,1)S(1)}, bf16[256,512]{1,0:T(8,128)(2,1)}, u32[]{:S(2)}) %copy-start.2) | copy-done | bytes 262168
  3.5 0.0 copy-start.3
  3.5 0.9 %copy-done.3 = bf16[256,512]{1,0:T(8,128)(2,1)S(1)} copy-done((bf16[256,512]{1,0:T(8,128)(2,1)S(1)}, bf16[256,512]{1,0:T(8,128)(2,1)}, u32[]{:S(2)}) %copy-start.3) | copy-done | bytes 262168
  4.4 0.0 copy-start.4
  4.4 31.7 %spread.1 = (bf16[1024,128]{1,0:T(8,128)(2,1)S(1)}, bf16[4096,128]{1,0:T(8,128)(2,1)S(1)}, bf16[4096,128]{1,0:T(8,128)(2,1)S(1)}, bf16[1024,128]{1,0:T(8,128)(2,1)S(1)}) custom-call(bf16[256,512]{1,0:T(8,128)(2,1)S(1)} %copy-done, bf16[256,512]{1,0:T(8,128)(2,1)S(1)} %copy-done.1, bf16[256,512]{1,0:T(8,128)(2,1)S(1)} %copy-done.2, ...), custom_call_target="tpu_custom_call" | custom-call | tf_op jit(solution)/shard_map/spread/pallas_call | solution.py:254
  36.2 0.0 copy-done.4
  36.2 11.7 %attention.1 = (bf16[1024,128]{1,0:T(8,128)(2,1)S(1)}, bf16[4096,128]{1,0:T(8,128)(2,1)S(1)}, bf16[4096,128]{1,0:T(8,128)(2,1)S(1)}) custom-call(s32[32,32]{1,0:T(8,128)S(1)} %copy-done.4, bf16[1024,128]{1,0:T(8,128)(2,1)S(1)} %get-tuple-element.10.q, bf16[1024,128]{1,0:T(8,128)(2,1)S(1)} %get-tuple-element.11.g, bf16[4096,128]{1,0:T(8,128)(2,1)S(1)} %get-tuple-element.12.k, ...), custom_call_target="tpu_custom_call" | custom-call | tf_op jit(solution)/shard_map/attention/pallas_call | solution.py:375
  47.9 29.4 %collect.1 = (bf16[256,512]{1,0:T(8,128)(2,1)S(1)}, bf16[256,512]{1,0:T(8,128)(2,1)S(1)}, bf16[256,512]{1,0:T(8,128)(2,1)S(1)}) custom-call(bf16[1024,128]{1,0:T(8,128)(2,1)S(1)} %get-tuple-element.14.dq_in, bf16[4096,128]{1,0:T(8,128)(2,1)S(1)} %get-tuple-element.15.dk_in, bf16[4096,128]{1,0:T(8,128)(2,1)S(1)} %get-tuple-element.16.dv_in), custom_call_target="tpu_custom_call" | custom-call | tf_op jit(solution)/shard_map/collect/pallas_call | solution.py:495
  77.3 0.7 copy.12
  78.0 0.7 copy.13
  78.7 0.7 copy.14
Async XLA Ops:
  0.6 1.0 %copy-start = (bf16[256,512]{1,0:T(8,128)(2,1)S(1)}, bf16[256,512]{1,0:T(8,128)(2,1)}, u32[]{:S(2)}) copy-start(bf16[256,512]{1,0:T(8,128)(2,1)} %q_in.1) | copy-start | bytes 786436
  1.6 0.9 %copy-start.1 = (bf16[256,512]{1,0:T(8,128)(2,1)S(1)}, bf16[256,512]{1,0:T(8,128)(2,1)}, u32[]{:S(2)}) copy-start(bf16[256,512]{1,0:T(8,128)(2,1)} %k_in.1) | copy-start | bytes 786436
  2.5 0.9 %copy-start.2 = (bf16[256,512]{1,0:T(8,128)(2,1)S(1)}, bf16[256,512]{1,0:T(8,128)(2,1)}, u32[]{:S(2)}) copy-start(bf16[256,512]{1,0:T(8,128)(2,1)} %v_in.1) | copy-start | bytes 786436
  3.5 0.9 %copy-start.3 = (bf16[256,512]{1,0:T(8,128)(2,1)S(1)}, bf16[256,512]{1,0:T(8,128)(2,1)}, u32[]{:S(2)}) copy-start(bf16[256,512]{1,0:T(8,128)(2,1)} %og_in.1) | copy-start | bytes 786436
  4.4 31.8 %copy-start.4 = (s32[32,32]{1,0:T(8,128)S(1)}, s32[32,32]{1,0:T(8,128)}, u32[]{:S(2)}) copy-start(s32[32,32]{1,0:T(8,128)} %mask.1) | copy-start | bytes 12292

commit v2 on v1

--- a/solution.py
+++ b/solution.py
@@ -298,7 +298,7 @@
             bias[1, count] = jnp.where(m1, 0.0, NEG_FILL)
             return count + jnp.where(m0 | m1, 1, 0)
 
-        count = lax.fori_loop(0, 32, pick, 0)
+        count = lax.fori_loop(0, 32, pick, 0, unroll=8)
         steps = lax.div(count + GROUP - 1, GROUP)
 
         def pad(b, carry):
@@ -516,10 +516,35 @@
     )(dq, dk, dv)
 
 
+def store_kernel(*refs):
+    ins, outs, sem = refs[:3], refs[3:6], refs[6]
+    copies = [pltpu.make_async_copy(a, b, sem.at[i]) for i, (a, b) in enumerate(zip(ins, outs))]
+    for copy in copies:
+        copy.start()
+    for copy in copies:
+        copy.wait()
+
+
+def store(dq, dk, dv):
+    anywhere = pl.BlockSpec(memory_space=pl.ANY)
+    return pl.pallas_call(
+        store_kernel,
+        out_shape=(jax.ShapeDtypeStruct((ROWS, 512), BF16),) * 3,
+        in_specs=[pl.BlockSpec(memory_space=pltpu.VMEM)] * 3,
+        out_specs=(anywhere,) * 3,
+        scratch_shapes=[pltpu.SemaphoreType.DMA((3,))],
+        name="store",
+    )(dq, dk, dv)
+
+
 def per_device(query_proj, key_proj, value_proj, out_grad, out_weight, block_mask):
+    query_proj, key_proj, value_proj, out_grad = [
+        pltpu.with_memory_space_constraint(a, pltpu.HBM)
+        for a in (query_proj, key_proj, value_proj, out_grad)
+    ]
     q, k, v, g = spread(query_proj, key_proj, value_proj, out_grad, out_weight)
     dq, dk, dv = attention(block_mask, q, g, k, v)
-    return collect(dq, dk, dv)
+    return store(*collect(dq, dk, dv))
 
 
 def solution(mesh):

time: 79.6 us -> 77.4 us (0.972)
  local copies, waits for them, and re-layouts: 5.9 us -> 2.1 us
  Pallas kernels: 72.8 us -> 74.5 us
    unnamed x13 -> x8, local copies, waits for them, and re-layouts: 5.9 us -> 2.1 us
    pallas_call x0 -> x1, Pallas kernels: none -> 2.01 us  [store(): pl.pallas_call(store_kernel, out_shape=(jax.ShapeDtypeStruct((ROWS, 512),...]
    pallas_call x1, Pallas kernels: 11.7 us -> 9.72 us  [attention(): pl.pallas_call(attention_kernel, out_shape=(jax.ShapeDtypeStruct((NX * RO...]
    pallas_call x1, Pallas kernels: 29.4 us -> 31 us  [collect(): pl.pallas_call(collect_kernel, out_shape=(jax.ShapeDtypeStruct((ROWS, 512...]
where the time goes in v2:
time: 77.4 us; the launch traced here: 77.3 us
  Pallas kernels  74.5 us (96%)
  local copies, waits for them, and re-layouts  2.1 us (3%)
    pallas_call x1, Pallas kernels, spread(): pl.pallas_call(spread_kernel, out_shape=(jax.ShapeDtypeStruct((NX * ROWS,...  31.8 us
    pallas_call x1, Pallas kernels, collect(): pl.pallas_call(collect_kernel, out_shape=(jax.ShapeDtypeStruct((ROWS, 512...  31 us
    pallas_call x1, Pallas kernels, attention(): pl.pallas_call(attention_kernel, out_shape=(jax.ShapeDtypeStruct((NX * RO...  9.72 us
    unnamed x8, local copies, waits for them, and re-layouts  2.1 us
    pallas_call x1, Pallas kernels, store(): pl.pallas_call(store_kernel, out_shape=(jax.ShapeDtypeStruct((ROWS, 512),...  2.01 us

profile of v2, /device:TPU:1, one launch (start us, length us, event | category | flops | bytes accessed | tf_op | source)
XLA Modules:
  0.0 77.3 jit_solution(2872664989320798606)
XLA Ops:
  0.6 0.0 copy-start.3
  0.6 31.8 %spread.1 = (bf16[1024,128]{1,0:T(8,128)(2,1)S(1)}, bf16[4096,128]{1,0:T(8,128)(2,1)S(1)}, bf16[4096,128]{1,0:T(8,128)(2,1)S(1)}, bf16[1024,128]{1,0:T(8,128)(2,1)S(1)}) custom-call(bf16[256,512]{1,0:T(8,128)(2,1)} %q_in.1, bf16[256,512]{1,0:T(8,128)(2,1)} %k_in.1, bf16[256,512]{1,0:T(8,128)(2,1)} %v_in.1, bf16[256,512]{1,0:T(8,128)(2,1)} %og_in.1, ...), custom_call_target="tpu_custom_call" | custom-call | tf_op jit(solution)/shard_map/spread/pallas_call | solution.py:254
  32.5 0.0 copy-done.3
  32.5 9.7 %attention.1 = (bf16[1024,128]{1,0:T(8,128)(2,1)S(1)}, bf16[4096,128]{1,0:T(8,128)(2,1)S(1)}, bf16[4096,128]{1,0:T(8,128)(2,1)S(1)}) custom-call(s32[32,32]{1,0:T(8,128)S(1)} %copy-done.3, bf16[1024,128]{1,0:T(8,128)(2,1)S(1)} %get-tuple-element.13.q, bf16[1024,128]{1,0:T(8,128)(2,1)S(1)} %get-tuple-element.14.g, bf16[4096,128]{1,0:T(8,128)(2,1)S(1)} %get-tuple-element.15.k, ...), custom_call_target="tpu_custom_call" | custom-call | tf_op jit(solution)/shard_map/attention/pallas_call | solution.py:375
  42.2 31.0 %collect.1 = (bf16[256,512]{1,0:T(8,128)(2,1)S(1)}, bf16[256,512]{1,0:T(8,128)(2,1)S(1)}, bf16[256,512]{1,0:T(8,128)(2,1)S(1)}) custom-call(bf16[1024,128]{1,0:T(8,128)(2,1)S(1)} %get-tuple-element.17.dq_in, bf16[4096,128]{1,0:T(8,128)(2,1)S(1)} %get-tuple-element.18.dk_in, bf16[4096,128]{1,0:T(8,128)(2,1)S(1)} %get-tuple-element.19.dv_in), custom_call_target="tpu_custom_call" | custom-call | tf_op jit(solution)/shard_map/collect/pallas_call | solution.py:495
  73.2 0.0 copy-start
  73.2 0.7 copy-done
  73.9 0.0 copy-start.1
  73.9 0.7 copy-done.1
  74.6 0.0 copy-start.2
  74.6 0.7 copy-done.2
  75.3 2.0 %store.1 = (bf16[256,512]{1,0:T(8,128)(2,1)}, bf16[256,512]{1,0:T(8,128)(2,1)}, bf16[256,512]{1,0:T(8,128)(2,1)}) custom-call(bf16[256,512]{1,0:T(8,128)(2,1)} %copy-done, bf16[256,512]{1,0:T(8,128)(2,1)} %copy-done.1, bf16[256,512]{1,0:T(8,128)(2,1)} %copy-done.2), custom_call_target="tpu_custom_call" | custom-call | tf_op jit(solution)/shard_map/store/pallas_call | solution.py:530
Async XLA Ops:
  0.6 31.8 %copy-start.3 = (s32[32,32]{1,0:T(8,128)S(1)}, s32[32,32]{1,0:T(8,128)}, u32[]{:S(2)}) copy-start(s32[32,32]{1,0:T(8,128)} %mask.1) | copy-start | bytes 12292
  73.2 0.7 copy-start
  73.9 0.7 copy-start.1
  74.6 0.7 copy-start.2

commit v3 on v2

--- a/solution.py
+++ b/solution.py
@@ -12,6 +12,7 @@
 BLOCK = 128
 ROWS = 256
 NX = 4
+NB = 32
 NEG_FILL = -1e30
 SCALE = HEAD_DIM ** (-0.5)
 LOG2E = 1.4426950408889634
@@ -49,10 +50,31 @@
     )
 
 
+def pick_blocks(mask, picks, zc):
+    down = lax.broadcasted_iota(jnp.int32, (NB, NB), 0)
+    across = lax.broadcasted_iota(jnp.int32, (NB, NB), 1)
+    upto = jnp.where(across <= down, 1.0, 0.0)
+    for i in range(NX):
+        first = (i * 4 + zc) * 2
+        may = [jnp.where(mask[pl.ds(first + a, 1), :] == 1, 1.0, 0.0) for a in range(2)]
+        either = jnp.broadcast_to(jnp.maximum(may[0], may[1]), (8, NB))
+        before = lax.dot_general(upto, either, NT, preferred_element_type=F32)[:, 0:1]
+        total = jnp.sum(either[0:1], axis=1, keepdims=True).astype(jnp.int32)
+        place_of = jnp.sum(
+            jnp.where(before.astype(jnp.int32) <= across, 1, 0), axis=0, keepdims=True)
+        at = across[0:1]
+        chosen = jnp.where((down == place_of) & (at < total), 1.0, 0.0)
+        picks[i:i + 1, :] = jnp.where(at < total, place_of, 0)
+        for a in range(2):
+            held = jnp.dot(jnp.broadcast_to(may[a], (8, NB)), chosen, preferred_element_type=F32)
+            picks[4 + 4 * a + i:5 + 4 * a + i, :] = held[0:1].astype(jnp.int32)
+        picks[12 + i:13 + i, :] = jnp.broadcast_to(total, (1, NB))
+
+
 def spread_kernel(
-    q_in, k_in, v_in, og_in, w_in,
-    q_out, k_out, v_out, g_out,
-    og, w, own, relay, relay_got, comb, comb_got, direct, direct_got, z_part, z_got, g_part,
+    q_in, k_in, v_in, og_in, w_in, mask_in,
+    q_out, k_out, v_out, g_out, picks,
+    mask, og, w, own, relay, relay_got, comb, comb_got, direct, direct_got, z_part, z_got, g_part,
     load_sem, local_sem, y_send, y_recv, z_send, z_recv, g_send, g_recv,
     q_send, q_recv, kv_xsend, kv_xrecv, kv_fsend, kv_frecv,
 ):
@@ -68,11 +90,13 @@
 
     order = [(yo, 0), (yo, 1), (yp, 0), (ym, 1), (yp, 1), (ym, 0), (y, 0), (y, 1)]
     loads = [pltpu.make_async_copy(og_in, og, load_sem.at[8])]
+    mask_load = pltpu.make_async_copy(mask_in, mask, load_sem.at[9])
     for i, (yy, zz) in enumerate(order):
         rows = pl.ds(pl.multiple_of((zz * 4 + yy) * 512, 512), 512)
         loads.append(pltpu.make_async_copy(w_in.at[rows], w.at[i], load_sem.at[i]))
     for load in loads:
         load.start()
+    mask_load.start()
 
     barrier = pltpu.get_barrier_semaphore()
     for peer in (at_x(1), at_x(2), at_x(3), core, zpeer, up, down, zfar):
@@ -210,6 +234,8 @@
             kv_wait(t, d, 1)
             go(kv_forward(t, d, 2))
 
+    mask_load.wait()
+    pick_blocks(mask, picks, z * 2 + c)
     combine(0)
     pass_on(1)
     combine(1)
@@ -248,9 +274,10 @@
         copy.wait_send()
 
 
-def spread(q, k, v, og, w):
+def spread(q, k, v, og, w, mask):
     dma = pltpu.SemaphoreType.DMA
     hbm = pl.BlockSpec(memory_space=pltpu.HBM)
+    vmem = pl.BlockSpec(memory_space=pltpu.VMEM)
     return pl.pallas_call(
         spread_kernel,
         out_shape=(
@@ -258,16 +285,18 @@
             jax.ShapeDtypeStruct((16 * ROWS, 128), BF16),
             jax.ShapeDtypeStruct((16 * ROWS, 128), BF16),
             jax.ShapeDtypeStruct((NX * ROWS, 128), BF16),
+            jax.ShapeDtypeStruct((16, NB), jnp.int32),
         ),
-        in_specs=[hbm] * 5,
-        out_specs=(hbm,) * 4,
+        in_specs=[hbm] * 6,
+        out_specs=(hbm,) * 4 + (vmem,),
         scratch_shapes=[
+            pltpu.VMEM((NB, NB), jnp.int32),
             pltpu.VMEM((ROWS, 512), BF16),
             pltpu.VMEM((8, 512, 512), BF16),
             pltpu.VMEM((2, 2, 4, ROWS, 128), F32),
             *[pltpu.VMEM((2, 4, ROWS, 128), BF16)] * 6,
             *[pltpu.VMEM((4, ROWS, 128), BF16)] * 3,
-            dma((9,)), dma((4,)),
+            dma((10,)), dma((4,)),
             dma((3, 2, 4)), dma((3, 2, 4)),
             dma((4,)), dma((4,)), dma((3,)), dma((3,)),
             dma((4,)), dma((4,)),
@@ -277,91 +306,82 @@
             collective_id=0, has_side_effects=True, vmem_limit_bytes=48 << 20
         ),
         name="spread",
-    )(q, k, v, og, w)
-
-
-GROUP = 4
-
-
-def attention_kernel(mask, q, g, k, v, dq, dk, dv, s_scr, p_scr, dk_acc, dv_acc, picks, bias):
-    ctx = lax.axis_index("ctx")
-    zc = lax.rem(ctx, 4)
+    )(q, k, v, og, w, mask)
+
+
+def attention_kernel(picks, q, g, k, v, dq, dk, dv, s_scr, p_scr, dk_acc, dv_acc):
     dk_acc[...] = jnp.zeros_like(dk_acc)
     dv_acc[...] = jnp.zeros_like(dv_acc)
 
     def tile(i, carry):
-        first = (i * 4 + zc) * 2
-        def pick(b, count):
-            m0, m1 = mask[first, b] == 1, mask[first + 1, b] == 1
-            picks[count] = b
-            bias[0, count] = jnp.where(m0, 0.0, NEG_FILL)
-            bias[1, count] = jnp.where(m1, 0.0, NEG_FILL)
-            return count + jnp.where(m0 | m1, 1, 0)
-
-        count = lax.fori_loop(0, 32, pick, 0, unroll=8)
-        steps = lax.div(count + GROUP - 1, GROUP)
-
-        def pad(b, carry):
-            picks[b] = 0
-            bias[0, b] = NEG_FILL
-            bias[1, b] = NEG_FILL
-            return carry
-
-        lax.fori_loop(count, steps * GROUP, pad, 0)
+        count = picks[12 + i, 0]
+        rest = lax.rem(count, 8)
+        wide = lax.div(count, 8) + jnp.where(rest > 4, 1, 0)
+        narrow = jnp.where((rest > 0) & (rest <= 4), 1, 0)
+
+        def steps(body, carry):
+            carry = lax.fori_loop(0, wide, lambda j, carry: body(8, j * 8, carry), carry)
+            return lax.fori_loop(0, narrow, lambda j, carry: body(4, wide * 8, carry), carry)
 
         q_rows = pl.ds(pl.multiple_of(i * ROWS, ROWS), ROWS)
         q_tile, g_tile = q[q_rows, :], g[q_rows, :]
 
-        def rows_of(j, n):
-            return pl.ds(pl.multiple_of(picks[j * GROUP + n] * BLOCK, BLOCK), BLOCK)
-
-        def scores(j, top):
-            k_cat = jnp.concatenate([k[rows_of(j, n), :] for n in range(GROUP)], axis=0)
-            v_cat = jnp.concatenate([v[rows_of(j, n), :] for n in range(GROUP)], axis=0)
-            s = lax.dot_general(k_cat, q_tile, NT, preferred_element_type=F32)
-            p_scr[j] = lax.dot_general(v_cat, g_tile, NT, preferred_element_type=F32)
-            for n in range(GROUP):
+        def rows_of(n):
+            return pl.ds(pl.multiple_of(picks[i, n] * BLOCK, BLOCK), BLOCK)
+
+        def gather(ref, size, base):
+            return jnp.concatenate([ref[rows_of(base + n), :] for n in range(size)], axis=0)
+
+        def fold(op, tall):
+            return op(tall.reshape(-1, 8, ROWS), axis=0)
+
+        def scores(size, base, top):
+            s = lax.dot_general(gather(k, size, base), q_tile, NT, preferred_element_type=F32)
+            prob_grad = lax.dot_general(gather(v, size, base), g_tile, NT, preferred_element_type=F32)
+            p_scr[pl.ds(base, size)] = prob_grad.reshape(size, BLOCK, ROWS)
+            for n in range(size):
                 fill = jnp.concatenate(
-                    [jnp.full((1, 128), bias[a, j * GROUP + n], F32) for a in range(2)], axis=1
+                    [
+                        jnp.full((1, 128), jnp.where(picks[4 + 4 * a + i, base + n] == 1, 0.0, NEG_FILL), F32)
+                        for a in range(2)
+                    ],
+                    axis=1,
                 )
                 part = s[n * BLOCK:(n + 1) * BLOCK] * (SCALE * LOG2E) + fill
-                s_scr[j, n * BLOCK:(n + 1) * BLOCK, :] = part
-                top = jnp.maximum(top, jnp.max(part.reshape(BLOCK // 8, 8, ROWS), axis=0))
+                s_scr[base + n] = part
+                top = jnp.maximum(top, fold(jnp.max, part))
             return top
 
-        top = lax.fori_loop(0, steps, scores, jnp.full((8, ROWS), NEG_FILL, F32))
+        top = steps(scores, jnp.full((8, ROWS), NEG_FILL, F32))
         top = jnp.max(top, axis=0, keepdims=True)
 
-        def sums(j, carry):
+        def sums(size, base, carry):
             total, weighted = carry
-            e = jnp.exp2(s_scr[j] - top)
-            s_scr[j] = e
-            total = total + jnp.sum(e.reshape(GROUP * BLOCK // 8, 8, ROWS), axis=0)
-            weighted = weighted + jnp.sum((e * p_scr[j]).reshape(GROUP * BLOCK // 8, 8, ROWS), axis=0)
-            return total, weighted
+            e = jnp.exp2(s_scr[pl.ds(base, size)] - top)
+            s_scr[pl.ds(base, size)] = e
+            return total + fold(jnp.sum, e), weighted + fold(jnp.sum, e * p_scr[pl.ds(base, size)])
 
         zero = jnp.zeros((8, ROWS), F32)
-        total, weighted = lax.fori_loop(0, steps, sums, (zero, zero))
+        total, weighted = steps(sums, (zero, zero))
         inverse = 1.0 / jnp.sum(total, axis=0, keepdims=True)
         delta = jnp.sum(weighted, axis=0, keepdims=True) * inverse
 
-        def grads(j, dq_acc):
-            p = s_scr[j] * inverse
-            ds = (p * (p_scr[j] - delta)).astype(BF16)
+        def grads(size, base, dq_acc):
+            p = s_scr[pl.ds(base, size)].reshape(size * BLOCK, ROWS) * inverse
+            ds = (p * (p_scr[pl.ds(base, size)].reshape(size * BLOCK, ROWS) - delta)).astype(BF16)
             p = p.astype(BF16)
-            k_cat = jnp.concatenate([k[rows_of(j, n), :] for n in range(GROUP)], axis=0)
             dv_part = jnp.dot(p, g_tile, preferred_element_type=F32)
             dk_part = jnp.dot(ds, q_tile, preferred_element_type=F32)
             dq_acc = dq_acc + lax.dot_general(
-                ds, k_cat, (((0,), (0,)), ((), ())), preferred_element_type=F32
+                ds, gather(k, size, base), (((0,), (0,)), ((), ())), preferred_element_type=F32
             )
-            for n in range(GROUP):
-                rows = rows_of(j, n)
+            for n in range(size):
+                rows = rows_of(base + n)
                 dk_acc[rows, :] += dk_part[n * BLOCK:(n + 1) * BLOCK]
                 dv_acc[rows, :] += dv_part[n * BLOCK:(n + 1) * BLOCK]
             return dq_acc
 
-        dq_acc = lax.fori_loop(0, steps, grads, jnp.zeros((ROWS, 128), F32))
+        dq_acc = steps(grads, jnp.zeros((ROWS, 128), F32))
         dq[q_rows, :] = (dq_acc * SCALE).astype(BF16)
         return carry
 
@@ -370,7 +390,7 @@
     dv[...] = dv_acc[...].astype(BF16)
 
 
-def attention(mask, q, g, k, v):
+def attention(picks, q, g, k, v):
     vmem = pl.BlockSpec(memory_space=pltpu.VMEM)
     return pl.pallas_call(
         attention_kernel,
@@ -382,16 +402,14 @@
         in_specs=[pl.BlockSpec(memory_space=pltpu.SMEM)] + [vmem] * 4,
         out_specs=(vmem,) * 3,
         scratch_shapes=[
-            pltpu.VMEM((32 // GROUP, GROUP * BLOCK, ROWS), F32),
-            pltpu.VMEM((32 // GROUP, GROUP * BLOCK, ROWS), F32),
+            pltpu.VMEM((NB, BLOCK, ROWS), F32),
+            pltpu.VMEM((NB, BLOCK, ROWS), F32),
             pltpu.VMEM((16 * ROWS, 128), F32),
             pltpu.VMEM((16 * ROWS, 128), F32),
-            pltpu.SMEM((64,), jnp.int32),
-            pltpu.SMEM((2, 64), F32),
         ],
         compiler_params=pltpu.CompilerParams(vmem_limit_bytes=48 << 20),
         name="attention",
-    )(mask, q, g, k, v)
+    )(picks, q, g, k, v)
 
 
 def collect_kernel(
@@ -530,20 +548,21 @@
     return pl.pallas_call(
         store_kernel,
         out_shape=(jax.ShapeDtypeStruct((ROWS, 512), BF16),) * 3,
-        in_specs=[pl.BlockSpec(memory_space=pltpu.VMEM)] * 3,
+        in_specs=[anywhere] * 3,
         out_specs=(anywhere,) * 3,
         scratch_shapes=[pltpu.SemaphoreType.DMA((3,))],
+        compiler_params=pltpu.CompilerParams(vmem_limit_bytes=16 << 20),
         name="store",
     )(dq, dk, dv)
 
 
 def per_device(query_proj, key_proj, value_proj, out_grad, out_weight, block_mask):
-    query_proj, key_proj, value_proj, out_grad = [
+    query_proj, key_proj, value_proj, out_grad, block_mask = [
         pltpu.with_memory_space_constraint(a, pltpu.HBM)
-        for a in (query_proj, key_proj, value_proj, out_grad)
+        for a in (query_proj, key_proj, value_proj, out_grad, block_mask)
     ]
-    q, k, v, g = spread(query_proj, key_proj, value_proj, out_grad, out_weight)
-    dq, dk, dv = attention(block_mask, q, g, k, v)
+    q, k, v, g, picks = spread(query_proj, key_proj, value_proj, out_grad, out_weight, block_mask)
+    dq, dk, dv = attention(picks, q, g, k, v)
     return store(*collect(dq, dk, dv))
 
 

time: 77.4 us -> 65.1 us (0.84)
  Pallas kernels: 74.5 us -> 64.3 us
  local copies, waits for them, and re-layouts: 2.1 us -> 0 us
    pallas_call x1, Pallas kernels: 31 us -> 24.5 us  [collect(): pl.pallas_call(collect_kernel, out_shape=(jax.ShapeDtypeStruct((ROWS, 512...]
    pallas_call x1, Pallas kernels: 9.72 us -> 7.07 us  [attention(): pl.pallas_call(attention_kernel, out_shape=(jax.ShapeDtypeStruct((NX * RO...]
    unnamed x8 -> x0, local copies, waits for them, and re-layouts: 2.1 us -> none
    pallas_call x1, Pallas kernels: 2.01 us -> 0.9 us  [store(): pl.pallas_call(store_kernel, out_shape=(jax.ShapeDtypeStruct((ROWS, 512),...]
where the time goes in v3:
time: 65.1 us; the launch traced here: 65 us
  Pallas kernels  64.3 us (99%)
  between operations  0.66 us (1%)
    pallas_call x1, Pallas kernels, spread(): pl.pallas_call(spread_kernel, out_shape=(jax.ShapeDtypeStruct((NX * ROWS,...  31.8 us
    pallas_call x1, Pallas kernels, collect(): pl.pallas_call(collect_kernel, out_shape=(jax.ShapeDtypeStruct((ROWS, 512...  24.5 us
    pallas_call x1, Pallas kernels, attention(): pl.pallas_call(attention_kernel, out_shape=(jax.ShapeDtypeStruct((NX * RO...  7.07 us

profile of v3, /device:TPU:1, one launch (start us, length us, event | category | flops | bytes accessed | tf_op | source)
XLA Modules:
  0.0 65.0 jit_solution(10982230215602365523)
XLA Ops:
  0.6 31.8 %spread.1 = (bf16[1024,128]{1,0:T(8,128)(2,1)S(1)}, bf16[4096,128]{1,0:T(8,128)(2,1)S(1)}, bf16[4096,128]{1,0:T(8,128)(2,1)S(1)}, bf16[1024,128]{1,0:T(8,128)(2,1)S(1)}, s32[16,32]{1,0:T(8,128)S(1)}) custom-call(bf16[256,512]{1,0:T(8,128)(2,1)} %q_in.1, bf16[256,512]{1,0:T(8,128)(2,1)} %k_in.1, bf16[256,512]{1,0:T(8,128)(2,1)} %v_in.1, ...), custom_call_target="tpu_custom_call" | custom-call | tf_op jit(solution)/shard_map/spread/pallas_call | solution.py:281
  32.5 7.1 %attention.1 = (bf16[1024,128]{1,0:T(8,128)(2,1)S(1)}, bf16[4096,128]{1,0:T(8,128)(2,1)S(1)}, bf16[4096,128]{1,0:T(8,128)(2,1)S(1)}) custom-call(s32[16,32]{1,0:T(8,128)S(1)} %get-tuple-element.14.picks, bf16[1024,128]{1,0:T(8,128)(2,1)S(1)} %get-tuple-element.15.q, bf16[1024,128]{1,0:T(8,128)(2,1)S(1)} %get-tuple-element.16.g, ...), custom_call_target="tpu_custom_call" | custom-call | tf_op jit(solution)/shard_map/attention/pallas_call | solution.py:395
  39.5 24.5 %collect.1 = (bf16[256,512]{1,0:T(8,128)(2,1)S(1)}, bf16[256,512]{1,0:T(8,128)(2,1)S(1)}, bf16[256,512]{1,0:T(8,128)(2,1)S(1)}) custom-call(bf16[1024,128]{1,0:T(8,128)(2,1)S(1)} %get-tuple-element.19.dq_in, bf16[4096,128]{1,0:T(8,128)(2,1)S(1)} %get-tuple-element.20.dk_in, bf16[4096,128]{1,0:T(8,128)(2,1)S(1)} %get-tuple-element.21.dv_in), custom_call_target="tpu_custom_call" | custom-call | tf_op jit(solution)/shard_map/collect/pallas_call | solution.py:513
  64.1 0.9 %store.1 = (bf16[256,512]{1,0:T(8,128)(2,1)}, bf16[256,512]{1,0:T(8,128)(2,1)}, bf16[256,512]{1,0:T(8,128)(2,1)}) custom-call(bf16[256,512]{1,0:T(8,128)(2,1)S(1)} %get-tuple-element.22.refs_0_, bf16[256,512]{1,0:T(8,128)(2,1)S(1)} %get-tuple-element.23.refs_1_, bf16[256,512]{1,0:T(8,128)(2,1)S(1)} %get-tuple-element.24.refs_2_), custom_call_target="tpu_custom_call" | custom-call | tf_op jit(solution)/shard_map/store/pallas_call | solution.py:548

commit v4 on v3

v4 whole, which is shorter than its diff:
```python
import functools

import jax
import jax.numpy as jnp
from jax import lax
from jax.experimental import pallas as pl
from jax.experimental.pallas import tpu as pltpu
from jax.sharding import PartitionSpec as P

MESH = pl.DeviceIdType.MESH
HEAD_DIM = 128
BLOCK = 128
ROWS = 256
NX = 4
NB = 32
NEG_FILL = -1e30
SCALE = HEAD_DIM ** (-0.5)
LOG2E = 1.4426950408889634
BF16 = jnp.bfloat16
F32 = jnp.float32
NT = (((1,), (1,)), ((), ()))


def place():
    ctx, tp = lax.axis_index("ctx"), lax.axis_index("tp")
    return (
        lax.div(ctx, 4),
        lax.rem(lax.div(ctx, 2), 2),
        lax.rem(ctx, 2),
        lax.div(tp, 4),
        lax.rem(tp, 4),
    )


def device(x, z, c, zh, y):
    return {"ctx": x * 4 + z * 2 + c, "tp": zh * 4 + y}


def block_rows(x, z, c):
    return pl.ds(pl.multiple_of((x * 4 + z * 2 + c) * ROWS, ROWS), ROWS)


def head_lanes(h):
    return pl.ds(pl.multiple_of(h * HEAD_DIM, HEAD_DIM), HEAD_DIM)


def remote(src, dst, send, recv, to):
    return pltpu.make_async_remote_copy(
        src_ref=src, dst_ref=dst, send_sem=send, recv_sem=recv, device_id=to, device_id_type=MESH
    )


def fill_table(mask, fill, zc):
    block = lax.broadcasted_iota(jnp.int32, (NB, NX * ROWS), 0)
    lane = lax.broadcasted_iota(jnp.int32, (NB, NX * ROWS), 1)
    query_block = ((lane >> 8) * 4 + zc) * 2 + ((lane >> 7) & 1)
    own = jnp.where(block == query_block, 1.0, 0.0)
    may = jnp.where(mask[...] == 1, 1.0, 0.0)
    held = lax.dot_general(may, own, (((0,), (0,)), ((), ())), preferred_element_type=F32)
    fill[...] = jnp.where(held > 0.5, 0.0, NEG_FILL)


def unit_scores(k_unit, q, fill, unit, shift):
    s = lax.dot_general(k_unit, q[...], NT, preferred_element_type=F32)
    count = k_unit.shape[0] // BLOCK
    parts = [
        s[a * BLOCK:(a + 1) * BLOCK] * (SCALE * LOG2E) + (fill[pl.ds(unit * count + a, 1), :] - shift)
        for a in range(count)
    ]
    return jnp.concatenate(parts, axis=0)


def start_totals(totals, out_t):
    row = lax.broadcasted_iota(jnp.int32, totals.shape, 0)
    totals[...] = jnp.where(row == 0, NEG_FILL, 0.0)
    out_t[...] = jnp.zeros_like(out_t)


def add_totals(k, v, q, fill, totals, out_t, unit):
    rows = pl.ds(pl.multiple_of(unit * 512, 512), 512)
    s = unit_scores(k[rows, :], q, fill, unit, 0.0)
    old = totals[0:1, :]
    new = jnp.maximum(old, jnp.max(s, axis=0, keepdims=True))
    e = jnp.exp2(s - new)
    keep = jnp.exp2(old - new)
    totals[0:1, :] = new
    totals[1:2, :] = totals[1:2, :] * keep + jnp.sum(e, axis=0, keepdims=True)
    v_t = jnp.concatenate([v[rows, :].T, jnp.ones((16, 512), BF16)], axis=0)
    out_t[...] = out_t[...] * keep + jnp.dot(v_t, e.astype(BF16), preferred_element_type=F32)


def end_totals(totals, out_t, log_total, mean_t):
    log_total[...] = totals[0:1, :] + jnp.log(totals[1:2, :]) * LOG2E
    mean_t[...] = out_t[0:128, :] * (1.0 / out_t[128:129, :])


def spread_kernel(
    q_in, k_in, v_in, og_in, w_in, mask_in,
    q_out, k_out, v_out, g_out, fill, log_total, mean_t,
    mask, totals, out_t, og, w, own, relay, relay_got, comb, comb_got, direct, direct_got, z_part, z_got, g_part,
    load_sem, local_sem, y_send, y_recv, z_send, z_recv, g_send, g_recv,
    q_send, q_recv, kv_xsend, kv_xrecv, kv_fsend, kv_frecv,
):
    x, z, c, zh, y = place()
    yp, ym, yo = lax.rem(y + 1, 4), lax.rem(y + 3, 4), lax.rem(y + 2, 4)

    def at_x(d):
        return device(lax.rem(x + d, 4), z, c, zh, y)

    core, zpeer = device(x, z, 1 - c, zh, y), device(x, 1 - z, c, zh, y)
    up, down = device(x, z, c, zh, yp), device(x, z, c, zh, ym)
    zfar = device(x, z, c, 1 - zh, y)

    order = [(yo, 0), (yo, 1), (yp, 0), (ym, 1), (yp, 1), (ym, 0), (y, 0), (y, 1)]
    loads = [pltpu.make_async_copy(og_in, og, load_sem.at[8])]
    mask_load = pltpu.make_async_copy(mask_in, mask, load_sem.at[9])
    for i, (yy, zz) in enumerate(order):
        rows = pl.ds(pl.multiple_of((zz * 4 + yy) * 512, 512), 512)
        loads.append(pltpu.make_async_copy(w_in.at[rows], w.at[i], load_sem.at[i]))
    for load in loads:
        load.start()
    mask_load.start()

    barrier = pltpu.get_barrier_semaphore()
    for peer in (at_x(1), at_x(2), at_x(3), core, zpeer, up, down, zfar):
        pl.semaphore_signal(barrier, inc=1, device_id=peer, device_id_type=MESH)
    pl.semaphore_wait(barrier, 8)

    sent = []

    def go(copy):
        copy.start()
        sent.append(copy)

    def project(i):
        loads[1 + i].wait()
        return lax.dot_general(og[...], w[i], NT, preferred_element_type=F32)

    heads = [lax.rem(x + 1 + i, 4) for i in range(4)]

    def y_copy(kind, zz, i, src, dst, to):
        return remote(
            src.at[zz, heads[i]], dst.at[zz, heads[i]],
            y_send.at[kind, zz, i], y_recv.at[kind, zz, i], to,
        )

    turns = [[y_copy(0, zz, i, relay, relay_got, (up, down)[zz]) for zz in range(2)] for i in range(4)]
    for i in range(4):
        turns.append([y_copy(1, zz, i, comb, comb_got, (up, down)[zz]) for zz in range(2)])
        turns.append([y_copy(2, zz, i, direct, direct_got, (down, up)[zz]) for zz in range(2)])

    def turn(n):
        for copy in turns[n]:
            go(copy)

    loads[0].wait()
    for zz in range(2):
        part = project(zz)
        for h in range(4):
            relay[zz, h] = part[:, h * 128:(h + 1) * 128].astype(BF16)
    for n in range(4):
        turn(n)

    tensors = [(k_in, k_out), (v_in, v_out)]

    def kv_from_x(t, d):
        src, dst = tensors[t]
        return remote(
            src.at[:, head_lanes(lax.rem(x + d, 4))], dst.at[block_rows(x, z, c)],
            kv_xsend.at[t, d], kv_xrecv.at[t, d], at_x(d),
        )

    def kv_wait_x(t, d):
        dst = tensors[t][1].at[block_rows(lax.rem(x + 4 - d, 4), z, c)]
        remote(dst, dst, kv_xsend.at[t, d], kv_xrecv.at[t, d], core).wait_recv()

    def kv_forward(t, d, route):
        xs = lax.rem(x + 4 - d, 4)
        rows = block_rows(xs, z if route < 2 else 1 - z, c)
        dst = tensors[t][1].at[rows]
        src = tensors[t][0].at[:, head_lanes(x)] if (d == 0 and route < 2) else dst
        return remote(
            src, dst, kv_fsend.at[t, d, route], kv_frecv.at[t, d, route], zpeer if route == 1 else core
        )

    def kv_wait(t, d, route):
        xs = lax.rem(x + 4 - d, 4)
        rows = block_rows(xs, z if route == 0 else 1 - z, c if route == 1 else 1 - c)
        dst = tensors[t][1].at[rows]
        remote(dst, dst, kv_fsend.at[t, d, route], kv_frecv.at[t, d, route], core).wait_recv()

    for t in range(2):
        go(kv_forward(t, 0, 1))
    for d in (1, 3, 2):
        for t in range(2):
            go(kv_from_x(t, d))
    for t in range(2):
        go(kv_forward(t, 0, 0))
    local = []
    for t in range(2):
        local.append(pltpu.make_async_copy(
            tensors[t][0].at[:, head_lanes(x)], tensors[t][1].at[block_rows(x, z, c)], local_sem.at[t]))
    q_rows = pl.ds(pl.multiple_of(x * ROWS, ROWS), ROWS)
    local.append(pltpu.make_async_copy(q_in.at[:, head_lanes(x)], q_out.at[q_rows], local_sem.at[2]))
    for copy in local:
        copy.start()
    q_copies = [
        remote(q_in.at[:, head_lanes(lax.rem(x + d, 4))], q_out.at[q_rows], q_send.at[d], q_recv.at[d], at_x(d))
        for d in (1, 2, 3)
    ]

    for i in range(2, 8):
        zz = order[i][1]
        part = project(i)
        for h in range(4):
            piece = part[:, h * 128:(h + 1) * 128]
            if i in (4, 5):
                direct[zz, h] = piece.astype(BF16)
            else:
                own[0 if i < 4 else 1, zz, h] = piece

    def combine(i):
        h = heads[i]
        for zz in range(2):
            turns[i][zz].wait_recv()
            comb[zz, h] = (relay_got[zz, h].astype(F32) + own[0, zz, h]).astype(BF16)

    z_copies = [
        remote(z_part.at[heads[i]], z_got.at[heads[i]], z_send.at[i], z_recv.at[i], zfar) for i in range(4)
    ]

    def finish_y(i):
        h = heads[i]
        for zz in range(2):
            y_copy(1, zz, i, comb, comb_got, up).wait_recv()
            y_copy(2, zz, i, direct, direct_got, up).wait_recv()
        far = own[1, 1 - zh, h] + comb_got[1 - zh, h].astype(F32) + direct_got[1 - zh, h].astype(F32)
        z_part[h] = far.astype(BF16)
        go(z_copies[i])
        own[1, zh, h] = own[1, zh, h] + comb_got[zh, h].astype(F32) + direct_got[zh, h].astype(F32)

    def finish_z(i):
        h = heads[i]
        z_copies[i].wait_recv()
        g_part[h] = (own[1, zh, h] + z_got[h].astype(F32)).astype(BF16)
        if i < 3:
            go(remote(g_part.at[h], g_out.at[q_rows], g_send.at[i], g_recv.at[i], at_x(i + 1)))
        else:
            copy = pltpu.make_async_copy(g_part.at[h], g_out.at[q_rows], local_sem.at[3])
            copy.start()
            local.append(copy)

    def pass_on(d):
        for t in range(2):
            kv_wait_x(t, d)
            go(kv_forward(t, d, 1))
            go(kv_forward(t, d, 0))

    def pass_z(d):
        for t in range(2):
            kv_wait(t, d, 1)
            go(kv_forward(t, d, 2))

    for copy in q_copies:
        go(copy)
    mask_load.wait()
    fill_table(mask, fill, z * 2 + c)
    start_totals(totals, out_t)
    for i in range(4):
        combine(i)
        turn(4 + 2 * i)
        turn(5 + 2 * i)
        if i < 3:
            pass_on((1, 3, 2)[i])

    def add_units(distances, zz):
        def one(i, carry):
            d = distances[0] + i * (distances[-1] - distances[0])
            add_totals(k_out, v_out, q_out, fill, totals, out_t, lax.rem(x + 8 - d, 4) * 2 + zz)
            return carry

        lax.fori_loop(0, len(distances), one, 0)

    def await_core(d, route):
        for t in range(2):
            kv_wait(t, d, route)

    for copy in q_copies:
        copy.wait_recv()
    for copy in local:
        copy.wait()
    local.clear()
    await_core(0, 0)
    await_core(1, 0)
    add_units((0, 1), z)
    finish_y(0)
    pass_z(0)
    await_core(3, 0)
    await_core(2, 0)
    add_units((3, 2), z)
    pass_z(1)
    finish_y(1)
    finish_z(0)
    await_core(0, 2)
    await_core(1, 2)
    add_units((0, 1), 1 - z)
    pass_z(3)
    pass_z(2)
    finish_y(2)
    finish_z(1)
    await_core(3, 2)
    await_core(2, 2)
    add_units((3, 2), 1 - z)
    end_totals(totals, out_t, log_total, mean_t)
    finish_y(3)
    finish_z(2)
    finish_z(3)

    for i in range(3):
        rows = pl.ds(pl.multiple_of(lax.rem(x + 3 - i, 4) * ROWS, ROWS), ROWS)
        dst = g_out.at[rows]
        remote(dst, dst, g_send.at[i], g_recv.at[i], core).wait_recv()
    for copy in local:
        copy.wait()
    for copy in sent:
        copy.wait_send()


def spread(q, k, v, og, w, mask):
    dma = pltpu.SemaphoreType.DMA
    hbm = pl.BlockSpec(memory_space=pltpu.HBM)
    vmem = pl.BlockSpec(memory_space=pltpu.VMEM)
    return pl.pallas_call(
        spread_kernel,
        out_shape=(
            jax.ShapeDtypeStruct((NX * ROWS, 128), BF16),
            jax.ShapeDtypeStruct((16 * ROWS, 128), BF16),
            jax.ShapeDtypeStruct((16 * ROWS, 128), BF16),
            jax.ShapeDtypeStruct((NX * ROWS, 128), BF16),
            jax.ShapeDtypeStruct((NB, NX * ROWS), F32),
            jax.ShapeDtypeStruct((1, NX * ROWS), F32),
            jax.ShapeDtypeStruct((128, NX * ROWS), F32),
        ),
        in_specs=[hbm] * 6,
        out_specs=(vmem,) * 7,
        scratch_shapes=[
            pltpu.VMEM((NB, NB), jnp.int32),
            pltpu.VMEM((8, NX * ROWS), F32),
            pltpu.VMEM((144, NX * ROWS), F32),
            pltpu.VMEM((ROWS, 512), BF16),
            pltpu.VMEM((8, 512, 512), BF16),
            pltpu.VMEM((2, 2, 4, ROWS, 128), F32),
            *[pltpu.VMEM((2, 4, ROWS, 128), BF16)] * 6,
            *[pltpu.VMEM((4, ROWS, 128), BF16)] * 3,
            dma((10,)), dma((4,)),
            dma((3, 2, 4)), dma((3, 2, 4)),
            dma((4,)), dma((4,)), dma((3,)), dma((3,)),
            dma((4,)), dma((4,)),
            dma((2, 4)), dma((2, 4)), dma((2, 4, 3)), dma((2, 4, 3)),
        ],
        compiler_params=pltpu.CompilerParams(
            collective_id=0, has_side_effects=True, vmem_limit_bytes=48 << 20
        ),
        name="spread",
    )(q, k, v, og, w, mask)


def backward_kernel(
    q, g, k, v, fill, log_total, mean_t,
    dq_out, dk_out, dv_out,
    delta, dq_t, dq_part,
    held, core_got, z_part, z_got, part,
    local_sem, core_send, core_recv, z_send, z_recv, x_send, x_recv, q_send, q_recv,
):
    x, z, c, zh, y = place()

    def at_x(d):
        return device(lax.rem(x + d, 4), z, c, zh, y)

    core, zpeer = device(x, z, 1 - c, zh, y), device(x, 1 - z, c, zh, y)
    outs = (dk_out, dv_out)

    barrier = pltpu.get_barrier_semaphore()
    for peer in (at_x(1), at_x(2), at_x(3), core, zpeer):
        pl.semaphore_signal(barrier, inc=1, device_id=peer, device_id_type=MESH)

    delta[...] = jnp.sum(mean_t[...] * g[...].T.astype(F32), axis=0, keepdims=True)
    dq_t[...] = jnp.zeros_like(dq_t)

    pl.semaphore_wait(barrier, 5)

    def unit_grads(unit, slot, mine):
        rows = pl.ds(pl.multiple_of(unit * ROWS, ROWS), ROWS)
        k_unit = k[rows, :]
        p = jnp.exp2(unit_scores(k_unit, q, fill, unit, log_total[...]))
        prob_grad = lax.dot_general(v[rows, :], g[...], NT, preferred_element_type=F32)
        ds = (p * (prob_grad - delta[...])).astype(BF16)
        held[slot, mine, 1] = jnp.dot(p.astype(BF16), g[...], preferred_element_type=F32).astype(BF16)
        held[slot, mine, 0] = (jnp.dot(ds, q[...], preferred_element_type=F32) * SCALE).astype(BF16)
        dq_t[...] += jnp.dot(k_unit.T, ds, preferred_element_type=F32)

    def core_copy(slot, t):
        return remote(
            held.at[slot, 0, t], core_got.at[slot, t], core_send.at[slot, t], core_recv.at[slot, t], core)

    def z_copy(i, t):
        return remote(z_part.at[i, t], z_got.at[i, t], z_send.at[i, t], z_recv.at[i, t], zpeer)

    def x_copy(i, t):
        return remote(
            part.at[i, t], outs[t].at[:, head_lanes(x)], x_send.at[i, t], x_recv.at[i, t], at_x(i + 1))

    def summed(slot, t):
        core_copy(slot, t).wait_recv()
        return held[slot, 1, t].astype(F32) + core_got[slot, t].astype(F32)

    def finish(i):
        for t in range(2):
            mine = summed(4 + i, t)
            z_copy(i, t).wait_recv()
            part[i, t] = (mine + z_got[i, t].astype(F32)).astype(BF16)

    def step(slot, carry):
        xx = lax.rem(x + 1 + slot, 4)
        zz = jnp.where(slot < 4, 1 - z, z)

        def half(mine, carry):
            unit_grads(xx * 4 + zz * 2 + jnp.where(mine == 0, 1 - c, c), slot, mine)

            @pl.when(mine == 0)
            def _():
                for t in range(2):
                    core_copy(slot, t).start()

            return carry

        lax.fori_loop(0, 2, half, 0)

        @pl.when(slot < 4)
        def _():
            for t in range(2):
                z_part[slot, t] = summed(slot, t).astype(BF16)
                z_copy(slot, t).start()

        @pl.when((slot >= 4) & (slot < 7))
        def _():
            finish(slot - 4)
            for t in range(2):
                x_copy(slot - 4, t).start()

        return carry

    lax.fori_loop(0, 8, step, 0)
    dq_part[...] = (dq_t[...] * SCALE).T.astype(BF16)

    def q_rows(xx):
        return pl.ds(pl.multiple_of(xx * ROWS, ROWS), ROWS)

    q_copies = [
        remote(
            dq_part.at[q_rows(lax.rem(x + d, 4))], dq_out.at[:, head_lanes(x)],
            q_send.at[d], q_recv.at[d], at_x(d))
        for d in (1, 2, 3)
    ]
    for copy in q_copies:
        copy.start()
    q_local = pltpu.make_async_copy(dq_part.at[q_rows(x)], dq_out.at[:, head_lanes(x)], local_sem.at[2])
    q_local.start()
    finish(3)
    for t in range(2):
        pltpu.make_async_copy(part.at[3, t], outs[t].at[:, head_lanes(x)], local_sem.at[t]).start()

    for i in range(3):
        lanes = head_lanes(lax.rem(x + 3 - i, 4))
        for t in range(2):
            dst = outs[t].at[:, lanes]
            remote(dst, dst, x_send.at[i, t], x_recv.at[i, t], core).wait_recv()
        dst = dq_out.at[:, lanes]
        remote(dst, dst, q_send.at[i + 1], q_recv.at[i + 1], core).wait_recv()
    q_local.wait()
    for t in range(2):
        pltpu.make_async_copy(part.at[3, t], outs[t].at[:, head_lanes(x)], local_sem.at[t]).wait()
        for i in range(3):
            x_copy(i, t).wait_send()
        for i in range(4):
            z_copy(i, t).wait_send()
        for slot in range(8):
            core_copy(slot, t).wait_send()
    for copy in q_copies:
        copy.wait_send()


def backward(*operands):
    dma = pltpu.SemaphoreType.DMA
    hbm = pl.BlockSpec(memory_space=pltpu.HBM)
    vmem = pl.BlockSpec(memory_space=pltpu.VMEM)
    piece = (2, ROWS, 128)
    lanes = NX * ROWS
    return pl.pallas_call(
        backward_kernel,
        out_shape=(jax.ShapeDtypeStruct((ROWS, 512), BF16),) * 3,
        in_specs=[vmem] * 7,
        out_specs=(hbm,) * 3,
        scratch_shapes=[
            pltpu.VMEM((1, lanes), F32),
            pltpu.VMEM((128, lanes), F32),
            pltpu.VMEM((lanes, 128), BF16),
            pltpu.VMEM((8, 2, *piece), BF16),
            pltpu.VMEM((8, *piece), BF16),
            *[pltpu.VMEM((4, *piece), BF16)] * 3,
            dma((3,)),
            dma((8, 2)), dma((8, 2)),
            dma((4, 2)), dma((4, 2)),
            dma((3, 2)), dma((3, 2)),
            dma((4,)), dma((4,)),
        ],
        compiler_params=pltpu.CompilerParams(
            collective_id=1, has_side_effects=True, vmem_limit_bytes=48 << 20
        ),
        name="backward",
    )(*operands)


def store_kernel(*refs):
    ins, outs, sem = refs[:3], refs[3:6], refs[6]
    copies = [pltpu.make_async_copy(a, b, sem.at[i]) for i, (a, b) in enumerate(zip(ins, outs))]
    for copy in copies:
        copy.start()
    for copy in copies:
        copy.wait()


def store(dq, dk, dv):
    anywhere = pl.BlockSpec(memory_space=pl.ANY)
    return pl.pallas_call(
        store_kernel,
        out_shape=(jax.ShapeDtypeStruct((ROWS, 512), BF16),) * 3,
        in_specs=[anywhere] * 3,
        out_specs=(anywhere,) * 3,
        scratch_shapes=[pltpu.SemaphoreType.DMA((3,))],
        compiler_params=pltpu.CompilerParams(vmem_limit_bytes=16 << 20),
        name="store",
    )(dq, dk, dv)


def per_device(query_proj, key_proj, value_proj, out_grad, out_weight, block_mask):
    query_proj, key_proj, value_proj, out_grad, block_mask = [
        pltpu.with_memory_space_constraint(a, pltpu.HBM)
        for a in (query_proj, key_proj, value_proj, out_grad, block_mask)
    ]
    q, k, v, g, fill, log_total, mean_t = spread(
        query_proj, key_proj, value_proj, out_grad, out_weight, block_mask
    )
    return store(*backward(q, g, k, v, fill, log_total, mean_t))


def solution(mesh):
    placed = (P("ctx", "tp"), P("ctx", "tp"), P("ctx", "tp"), P("ctx", "tp"), P(None, "tp"), P())
    return jax.shard_map(
        per_device,
        mesh=mesh,
        in_specs=placed,
        out_specs=(P("ctx", "tp"), P("ctx", "tp"), P("ctx", "tp")),
        check_vma=False,
    )
```

time: 65.1 us -> 62.4 us (0.959)
  Pallas kernels: 64.3 us -> 61.7 us
    pallas_call x2 -> x1, Pallas kernels: 31.6 us -> 25 us  [backward(): pl.pallas_call(backward_kernel, out_shape=(jax.ShapeDtypeStruct((ROWS, 51...]
    pallas_call x1, Pallas kernels: 31.8 us -> 35.8 us  [spread(): pl.pallas_call(spread_kernel, out_shape=(jax.ShapeDtypeStruct((NX * ROWS,...]
where the time goes in v4:
time: 62.4 us; the launch traced here: 62.3 us
  Pallas kernels  61.7 us (99%)
  between operations  0.65 us (1%)
    pallas_call x1, Pallas kernels, spread(): pl.pallas_call(spread_kernel, out_shape=(jax.ShapeDtypeStruct((NX * ROWS,...  35.8 us
    pallas_call x1, Pallas kernels, backward(): pl.pallas_call(backward_kernel, out_shape=(jax.ShapeDtypeStruct((ROWS, 51...  25 us

profile of v4, /device:TPU:1, one launch (start us, length us, event | category | flops | bytes accessed | tf_op | source)
XLA Modules:
  0.0 62.3 jit_solution(10114701952607464869)
XLA Ops:
  0.6 35.8 %spread.1 = (bf16[1024,128]{1,0:T(8,128)(2,1)S(1)}, bf16[4096,128]{1,0:T(8,128)(2,1)S(1)}, bf16[4096,128]{1,0:T(8,128)(2,1)S(1)}, bf16[1024,128]{1,0:T(8,128)(2,...) custom-call(bf16[256,512]{1,0:T(8,128)(2,1)} %q_in.1, bf16[256,512]{1,0:T(8,128)(2,1)} %k_in.1, ...), custom_call_target="tpu_custom_call" | custom-call | tf_op jit(solution)/shard_map/spread/pallas_call | solution.py:333
  36.4 25.0 %backward.1 = (bf16[256,512]{1,0:T(8,128)(2,1)S(1)}, bf16[256,512]{1,0:T(8,128)(2,1)S(1)}, bf16[256,512]{1,0:T(8,128)(2,1)S(1)}) custom-call(bf16[1024,128]{1,0:T(8,128)(2,1)S(1)} %get-tuple-element.13.q, bf16[1024,128]{1,0:T(8,128)(2,1)S(1)} %get-tuple-element.14.g, bf16[4096,128]{1,0:T(8,128)(2,1)S(1)} %get-tuple-element.15.k, ...), custom_call_target="tpu_custom_call" | custom-call | tf_op jit(solution)/shard_map/backward/pallas_call | solution.py:499
  61.4 0.9 %store.1 = (bf16[256,512]{1,0:T(8,128)(2,1)}, bf16[256,512]{1,0:T(8,128)(2,1)}, bf16[256,512]{1,0:T(8,128)(2,1)}) custom-call(bf16[256,512]{1,0:T(8,128)(2,1)S(1)} %get-tuple-element.20.refs_0_, bf16[256,512]{1,0:T(8,128)(2,1)S(1)} %get-tuple-element.21.refs_1_, bf16[256,512]{1,0:T(8,128)(2,1)S(1)} %get-tuple-element.22.refs_2_), custom_call_target="tpu_custom_call" | custom-call | tf_op jit(solution)/shard_map/store/pallas_call | solution.py:535

commit v5 on v4

--- a/solution.py
+++ b/solution.py
@@ -279,7 +279,7 @@
             add_totals(k_out, v_out, q_out, fill, totals, out_t, lax.rem(x + 8 - d, 4) * 2 + zz)
             return carry
 
-        lax.fori_loop(0, len(distances), one, 0)
+        lax.fori_loop(0, len(distances), one, 0, unroll=True)
 
     def await_core(d, route):
         for t in range(2):
@@ -434,7 +434,7 @@
 
             return carry
 
-        lax.fori_loop(0, 2, half, 0)
+        lax.fori_loop(0, 2, half, 0, unroll=True)
 
         @pl.when(slot < 4)
         def _():
@@ -442,7 +442,7 @@
                 z_part[slot, t] = summed(slot, t).astype(BF16)
                 z_copy(slot, t).start()
 
-        @pl.when((slot >= 4) & (slot < 7))
+        @pl.when(slot >= 4)
         def _():
             finish(slot - 4)
             for t in range(2):
@@ -450,8 +450,7 @@
 
         return carry
 
-    lax.fori_loop(0, 8, step, 0)
-    dq_part[...] = (dq_t[...] * SCALE).T.astype(BF16)
+    lax.fori_loop(0, 7, step, 0)
 
     def q_rows(xx):
         return pl.ds(pl.multiple_of(xx * ROWS, ROWS), ROWS)
@@ -462,10 +461,39 @@
             q_send.at[d], q_recv.at[d], at_x(d))
         for d in (1, 2, 3)
     ]
-    for copy in q_copies:
-        copy.start()
     q_local = pltpu.make_async_copy(dq_part.at[q_rows(x)], dq_out.at[:, head_lanes(x)], local_sem.at[2])
-    q_local.start()
+
+    last = x * 2 + z
+    last_rows = pl.ds(pl.multiple_of(last * 512, 512), 512)
+    k_last, v_last = k[last_rows, :], v[last_rows, :]
+    k_last_t = k_last.T
+    sums = [0.0, 0.0]
+    for j in range(4):
+        tile = q_rows(lax.rem(x + 1 + j, 4))
+        q_tile, g_tile = q[tile, :], g[tile, :]
+        s = lax.dot_general(k_last, q_tile, NT, preferred_element_type=F32)
+        p = jnp.exp2(jnp.concatenate(
+            [
+                s[a * BLOCK:(a + 1) * BLOCK] * (SCALE * LOG2E)
+                + (fill[pl.ds(last * 4 + a, 1), tile] - log_total[:, tile])
+                for a in range(4)
+            ],
+            axis=0,
+        ))
+        prob_grad = lax.dot_general(v_last, g_tile, NT, preferred_element_type=F32)
+        ds = (p * (prob_grad - delta[:, tile])).astype(BF16)
+        dq_tile = (dq_t[:, tile] + jnp.dot(k_last_t, ds, preferred_element_type=F32)) * SCALE
+        dq_part[tile, :] = dq_tile.T.astype(BF16)
+        if j < 3:
+            q_copies[j].start()
+        else:
+            q_local.start()
+        sums[0] += jnp.dot(ds, q_tile, preferred_element_type=F32)
+        sums[1] += jnp.dot(p.astype(BF16), g_tile, preferred_element_type=F32)
+    for t, total in enumerate((sums[0] * SCALE, sums[1])):
+        held[7, 1 - c, t] = total[:ROWS].astype(BF16)
+        held[7, c, t] = total[ROWS:].astype(BF16)
+        core_copy(7, t).start()
     finish(3)
     for t in range(2):
         pltpu.make_async_copy(part.at[3, t], outs[t].at[:, head_lanes(x)], local_sem.at[t]).start()

time: 62.4 us -> 61.6 us (0.987)
  Pallas kernels: 61.7 us -> 60.7 us
    pallas_call x1, Pallas kernels: 25 us -> 23.9 us  [backward(): pl.pallas_call(backward_kernel, out_shape=(jax.ShapeDtypeStruct((ROWS, 51...]
where the time goes in v5:
time: 61.6 us; the launch traced here: 61.5 us
  Pallas kernels  60.7 us (99%)
  between operations  0.81 us (1%)
    pallas_call x1, Pallas kernels, spread(): pl.pallas_call(spread_kernel, out_shape=(jax.ShapeDtypeStruct((NX * ROWS,...  35.9 us
    pallas_call x1, Pallas kernels, backward(): pl.pallas_call(backward_kernel, out_shape=(jax.ShapeDtypeStruct((ROWS, 51...  23.9 us

profile of v5, /device:TPU:1, one launch (start us, length us, event | category | flops | bytes accessed | tf_op | source)
XLA Modules:
  0.0 61.5 jit_solution(2195155463965250138)
XLA Ops:
  0.6 35.9 %spread.1 = (bf16[1024,128]{1,0:T(8,128)(2,1)S(1)}, bf16[4096,128]{1,0:T(8,128)(2,1)S(1)}, bf16[4096,128]{1,0:T(8,128)(2,1)S(1)}, bf16[1024,128]{1,0:T(8,128)(2,...) custom-call(bf16[256,512]{1,0:T(8,128)(2,1)} %q_in.1, bf16[256,512]{1,0:T(8,128)(2,1)} %k_in.1, ...), custom_call_target="tpu_custom_call" | custom-call | tf_op jit(solution)/shard_map/spread/pallas_call | solution.py:333
  36.6 23.9 %backward.1 = (bf16[256,512]{1,0:T(8,128)(2,1)S(1)}, bf16[256,512]{1,0:T(8,128)(2,1)S(1)}, bf16[256,512]{1,0:T(8,128)(2,1)S(1)}) custom-call(bf16[1024,128]{1,0:T(8,128)(2,1)S(1)} %get-tuple-element.13.q, bf16[1024,128]{1,0:T(8,128)(2,1)S(1)} %get-tuple-element.14.g, bf16[4096,128]{1,0:T(8,128)(2,1)S(1)} %get-tuple-element.15.k, ...), custom_call_target="tpu_custom_call" | custom-call | tf_op jit(solution)/shard_map/backward/pallas_call | solution.py:527
  60.4 0.9 %store.1 = (bf16[256,512]{1,0:T(8,128)(2,1)}, bf16[256,512]{1,0:T(8,128)(2,1)}, bf16[256,512]{1,0:T(8,128)(2,1)}) custom-call(bf16[256,512]{1,0:T(8,128)(2,1)S(1)} %get-tuple-element.20.refs_0_, bf16[256,512]{1,0:T(8,128)(2,1)S(1)} %get-tuple-element.21.refs_1_, bf16[256,512]{1,0:T(8,128)(2,1)S(1)} %get-tuple-element.22.refs_2_), custom_call_target="tpu_custom_call" | custom-call | tf_op jit(solution)/shard_map/store/pallas_call | solution.py:563

commit v6 on v5

--- a/solution.py
+++ b/solution.py
@@ -309,11 +309,12 @@
     finish_y(2)
     finish_z(1)
     await_core(3, 2)
-    await_core(2, 2)
-    add_units((3, 2), 1 - z)
-    end_totals(totals, out_t, log_total, mean_t)
+    add_units((3,), 1 - z)
     finish_y(3)
     finish_z(2)
+    await_core(2, 2)
+    add_units((2,), 1 - z)
+    end_totals(totals, out_t, log_total, mean_t)
     finish_z(3)
 
     for i in range(3):

time: 61.6 us -> 61 us (level)
    pallas_call x1, Pallas kernels: 35.9 us -> 34.8 us  [spread(): pl.pallas_call(spread_kernel, out_shape=(jax.ShapeDtypeStruct((NX * ROWS,...]
where the time goes in v6:
time: 61 us; the launch traced here: 60.9 us
  Pallas kernels  60.1 us (99%)
  between operations  0.81 us (1%)
    pallas_call x1, Pallas kernels, spread(): pl.pallas_call(spread_kernel, out_shape=(jax.ShapeDtypeStruct((NX * ROWS,...  34.8 us
    pallas_call x1, Pallas kernels, backward(): pl.pallas_call(backward_kernel, out_shape=(jax.ShapeDtypeStruct((ROWS, 51...  24.4 us

profile of v6, /device:TPU:1, one launch (start us, length us, event | category | flops | bytes accessed | tf_op | source)
XLA Modules:
  0.0 60.9 jit_solution(5848522554105482977)
XLA Ops:
  0.6 34.8 %spread.1 = (bf16[1024,128]{1,0:T(8,128)(2,1)S(1)}, bf16[4096,128]{1,0:T(8,128)(2,1)S(1)}, bf16[4096,128]{1,0:T(8,128)(2,1)S(1)}, bf16[1024,128]{1,0:T(8,128)(2,...) custom-call(bf16[256,512]{1,0:T(8,128)(2,1)} %q_in.1, bf16[256,512]{1,0:T(8,128)(2,1)} %k_in.1, ...), custom_call_target="tpu_custom_call" | custom-call | tf_op jit(solution)/shard_map/spread/pallas_call | solution.py:334
  35.4 24.4 %backward.1 = (bf16[256,512]{1,0:T(8,128)(2,1)S(1)}, bf16[256,512]{1,0:T(8,128)(2,1)S(1)}, bf16[256,512]{1,0:T(8,128)(2,1)S(1)}) custom-call(bf16[1024,128]{1,0:T(8,128)(2,1)S(1)} %get-tuple-element.13.q, bf16[1024,128]{1,0:T(8,128)(2,1)S(1)} %get-tuple-element.14.g, bf16[4096,128]{1,0:T(8,128)(2,1)S(1)} %get-tuple-element.15.k, ...), custom_call_target="tpu_custom_call" | custom-call | tf_op jit(solution)/shard_map/backward/pallas_call | solution.py:528
  59.8 0.9 %store.1 = (bf16[256,512]{1,0:T(8,128)(2,1)}, bf16[256,512]{1,0:T(8,128)(2,1)}, bf16[256,512]{1,0:T(8,128)(2,1)}) custom-call(bf16[256,512]{1,0:T(8,128)(2,1)S(1)} %get-tuple-element.20.refs_0_, bf16[256,512]{1,0:T(8,128)(2,1)S(1)} %get-tuple-element.21.refs_1_, bf16[256,512]{1,0:T(8,128)(2,1)S(1)} %get-tuple-element.22.refs_2_), custom_call_target="tpu_custom_call" | custom-call | tf_op jit(solution)/shard_map/store/pallas_call | solution.py:564
